TPU v7x, 32 devices: a whole 2x2x4 slice. The times are simulated.
32 devices in a mesh: shard: 8 (over z, y), rep: 4 (over x, core).
Axes of the slice: x: 2, y: 2, z: 4, core: 2. Of those that a mesh axis runs over, the one named last changes fastest.
Arguments:
- tokens: bfloat16 [64, 512, 768], P(('shard', 'rep')), may hold values from -6 to 6
- lengths: int32 [64], P(('shard', 'rep')), may hold values from 1 to 512, 20480 in all
- w_qkv: bfloat16 [768, 2304], P('shard'), may hold values from -0.21875 to 0.21875
- b_query: bfloat16 [768], P('shard'), may hold values from -3 to 3
- b_value: bfloat16 [768], P('shard'), may hold values from -3 to 3
- w_out: bfloat16 [768, 768], P('shard'), may hold values from -0.625 to 0.625
- b_out: bfloat16 [768], P('shard'), may hold values from -3 to 3
- ln1_gain: bfloat16 [768], P('shard'), may hold values from 0.5 to 1.5
- ln1_bias: bfloat16 [768], P('shard'), may hold values from -3 to 3
- w_up: bfloat16 [768, 3072], P('shard'), may hold values from -0.21875 to 0.21875
- b_up: bfloat16 [3072], P('shard'), may hold values from -3 to 3
- w_down: bfloat16 [3072, 768], P('shard'), may hold values from -0.109375 to 0.109375
- b_down: bfloat16 [768], P('shard'), may hold values from -3 to 3
- ln2_gain: bfloat16 [768], P('shard'), may hold values from 0.5 to 1.5
- ln2_bias: bfloat16 [768], P('shard'), may hold values from -3 to 3
- cotangent: bfloat16 [64, 512, 768], P(('shard', 'rep')), may hold values from -6 to 6
Outputs:
- layer_out: bfloat16 [64, 512, 768], P(('shard', 'rep'))
- input_grad: float32 [64, 512, 768], P(('shard', 'rep'))
- grad_w_qkv: float32 [768, 2304], P('shard')
- grad_b_query: float32 [768], P('shard')
- grad_b_value: float32 [768], P('shard')
- grad_w_out: float32 [768, 768], P('shard')
- grad_b_out: float32 [768], P('shard')
- grad_ln1_gain: float32 [768], P('shard')
- grad_ln1_bias: float32 [768], P('shard')
- grad_w_up: float32 [768, 3072], P('shard')
- grad_b_up: float32 [3072], P('shard')
- grad_w_down: float32 [3072, 768], P('shard')
- grad_b_down: float32 [768], P('shard')
- grad_ln2_gain: float32 [768], P('shard')
- grad_ln2_bias: float32 [768], P('shard')
Inputs may be any that keep to these rules, and one draw needn't show every extreme that they name: `lengths`: each sequence has at least one token; they add up to 64 * 512 * 5 // 8 tokens, and the longest has exactly 512.
All inputs are finite; a program needn't handle non-finite values. No bound on the sum of `lengths` on one device may be relied on, other than what follows from the above.
Results may differ from a plain program's by a relative error of at most 0.017.
Values may be sent and summed in bfloat16 or wider, within the bound.
No kernel may reach another device: no remote copies, remote signals or barrier semaphores. Data moves between devices by JAX's collectives and lax.ppermute only.
A program may use at most 192 MiB of HBM per device.

v0:
```python
import jax
import jax.numpy as jnp
from jax import lax
from jax.sharding import PartitionSpec as P

HEADS = 12


EPS = 1e-05


def layer_norm(hidden, gain, shift):
    center = hidden - jnp.mean(hidden, axis=-1, keepdims=True)
    spread = jnp.mean(center * center, axis=-1, keepdims=True)
    return center * lax.rsqrt(spread + EPS) * gain + shift


def gelu_exact(hidden):
    return jax.nn.gelu(hidden, approximate=False)


def inner_rows(left, right):
    return lax.dot_general(
        left, right, (((0,), (0,)), ((), ())), preferred_element_type=jnp.float32
    )


def times_back(left, right):
    return lax.dot_general(
        left, right, (((1,), (1,)), ((), ())), preferred_element_type=jnp.float32
    )


def split_heads(qkv_rows):
    length = qkv_rows.shape[0]
    head_dim = qkv_rows.shape[1] // (3 * HEADS)
    split = qkv_rows.reshape(length, 3, HEADS, head_dim)
    return (split[:, 0], split[:, 1], split[:, 2], head_dim)


def masked_scores(query_rows, key_rows, valid, head_dim):
    scores = jnp.einsum(
        "qhd,khd->hqk", query_rows, key_rows, preferred_element_type=jnp.float32
    ) * head_dim ** (-0.5)
    return jnp.where(valid[None, None, :], scores, -1e30)


def attend_forward(packed):
    qkv_rows, valid = packed
    length = qkv_rows.shape[0]
    query_rows, key_rows, value_rows, head_dim = split_heads(qkv_rows)
    scores = masked_scores(query_rows, key_rows, valid, head_dim)
    top = jnp.max(scores, axis=-1, keepdims=True)
    exp_scores = jnp.exp(scores - top)
    total = jnp.sum(exp_scores, axis=-1, keepdims=True)
    attn_prob = (exp_scores / total).astype(jnp.bfloat16)
    mixed = jnp.einsum("hqk,khd->qhd", attn_prob, value_rows, preferred_element_type=jnp.float32)
    log_total = top[..., 0] + jnp.log(total[..., 0])
    return (mixed.reshape(length, HEADS * head_dim), log_total)


def attend_back(packed):
    qkv_rows, grad_mixed, log_total, valid = packed
    length = qkv_rows.shape[0]
    query_rows, key_rows, value_rows, head_dim = split_heads(qkv_rows)
    scores = masked_scores(query_rows, key_rows, valid, head_dim)
    attn_prob = jnp.exp(scores - log_total[..., None])
    grad_heads = grad_mixed.reshape(length, HEADS, head_dim)
    grad_value = jnp.einsum(
        "hqk,qhd->khd",
        attn_prob.astype(jnp.bfloat16),
        grad_heads,
        preferred_element_type=jnp.float32,
    )
    grad_prob = jnp.einsum(
        "qhd,khd->hqk", grad_heads, value_rows, preferred_element_type=jnp.float32
    )
    grad_scores = attn_prob * (grad_prob - jnp.sum(attn_prob * grad_prob, axis=-1, keepdims=True))
    grad_low = grad_scores.astype(jnp.bfloat16)
    factor = head_dim ** (-0.5)
    grad_query = (
        jnp.einsum("hqk,khd->qhd", grad_low, key_rows, preferred_element_type=jnp.float32) * factor
    )
    grad_key = (
        jnp.einsum("hqk,qhd->khd", grad_low, query_rows, preferred_element_type=jnp.float32)
        * factor
    )
    stacked = jnp.stack([grad_query, grad_key, grad_value], axis=1)
    return stacked.reshape(length, 3 * HEADS * head_dim).astype(jnp.bfloat16)


def local(
    tokens,
    lengths,
    w_qkv,
    b_query,
    b_value,
    w_out,
    b_out,
    ln1_gain,
    ln1_bias,
    w_up,
    b_up,
    w_down,
    b_down,
    ln2_gain,
    ln2_bias,
    cotangent,
):
    attn_full = (
        lax.all_gather(w_qkv, "shard", axis=0, tiled=True),
        lax.all_gather(b_query, "shard", axis=0, tiled=True),
        lax.all_gather(b_value, "shard", axis=0, tiled=True),
        lax.all_gather(w_out, "shard", axis=0, tiled=True),
        lax.all_gather(b_out, "shard", axis=0, tiled=True),
        lax.all_gather(ln1_gain, "shard", axis=0, tiled=True),
        lax.all_gather(ln1_bias, "shard", axis=0, tiled=True),
    )
    ffn_full = (
        lax.all_gather(w_up, "shard", axis=0, tiled=True),
        lax.all_gather(b_up, "shard", axis=0, tiled=True),
        lax.all_gather(w_down, "shard", axis=0, tiled=True),
        lax.all_gather(b_down, "shard", axis=0, tiled=True),
        lax.all_gather(ln2_gain, "shard", axis=0, tiled=True),
        lax.all_gather(ln2_bias, "shard", axis=0, tiled=True),
    )
    seq_count, seq_len, width = tokens.shape
    total_rows = seq_count * seq_len
    valid = lax.broadcasted_iota(jnp.int32, (seq_count, seq_len), 1) < lengths[:, None]
    row_mask = valid.reshape(total_rows, 1)
    x_rows = tokens.reshape(total_rows, width)
    qkv_weight, query_bias, value_bias, out_weight, out_bias, gain_one, shift_one = attn_full
    bias = jnp.concatenate(
        [
            query_bias.astype(jnp.float32),
            jnp.zeros((width,), jnp.float32),
            value_bias.astype(jnp.float32),
        ]
    )
    qkv_rows = (jnp.dot(x_rows, qkv_weight, preferred_element_type=jnp.float32) + bias).astype(
        jnp.bfloat16
    )
    qkv_seqs = qkv_rows.reshape(seq_count, seq_len, 3 * width)
    mixed, log_total = lax.map(attend_forward, (qkv_seqs, valid))
    mixed_low = mixed.reshape(total_rows, width).astype(jnp.bfloat16)
    branch = jnp.dot(mixed_low, out_weight, preferred_element_type=jnp.float32) + out_bias.astype(
        jnp.float32
    )
    normed, norm_one_pull = jax.vjp(
        layer_norm,
        tokens.reshape(total_rows, width).astype(jnp.float32) + branch,
        gain_one.astype(jnp.float32),
        shift_one.astype(jnp.float32),
    )
    normed_low = normed.astype(jnp.bfloat16)
    up_weight, up_bias, down_weight, down_bias, gain_two, shift_two = ffn_full
    hidden = jnp.dot(normed_low, up_weight, preferred_element_type=jnp.float32) + up_bias.astype(
        jnp.float32
    )
    active, gelu_pull = jax.vjp(gelu_exact, hidden)
    active_low = active.astype(jnp.bfloat16)
    second = jnp.dot(
        active_low, down_weight, preferred_element_type=jnp.float32
    ) + down_bias.astype(jnp.float32)
    result, norm_two_pull = jax.vjp(
        layer_norm, normed + second, gain_two.astype(jnp.float32), shift_two.astype(jnp.float32)
    )
    result = jnp.where(row_mask, result, 0.0)
    layer_out = result.astype(jnp.bfloat16).reshape(seq_count, seq_len, width)
    ffn_back = (
        lax.all_gather(w_up, "shard", axis=0, tiled=True),
        lax.all_gather(b_up, "shard", axis=0, tiled=True),
        lax.all_gather(w_down, "shard", axis=0, tiled=True),
        lax.all_gather(b_down, "shard", axis=0, tiled=True),
        lax.all_gather(ln2_gain, "shard", axis=0, tiled=True),
        lax.all_gather(ln2_bias, "shard", axis=0, tiled=True),
    )
    up_weight, up_bias, down_weight, down_bias, gain_two, shift_two = ffn_back
    grad_result = jnp.where(row_mask, cotangent.reshape(total_rows, width).astype(jnp.float32), 0.0)
    grad_two, grad_gain_two, grad_shift_two = norm_two_pull(grad_result)
    grad_second = grad_two.astype(jnp.bfloat16)
    grad_down_bias = jnp.sum(grad_second.astype(jnp.float32), axis=0)
    grad_down = inner_rows(active_low, grad_second)
    grad_active = times_back(grad_second, down_weight)
    grad_hidden = gelu_pull(grad_active)[0].astype(jnp.bfloat16)
    grad_up_bias = jnp.sum(grad_hidden.astype(jnp.float32), axis=0)
    grad_up = inner_rows(normed_low, grad_hidden)
    grad_normed = grad_two + times_back(grad_hidden, up_weight)
    ffn_part = (
        lax.psum_scatter(grad_up, "shard", scatter_dimension=0, tiled=True),
        lax.psum_scatter(grad_up_bias, "shard", scatter_dimension=0, tiled=True),
        lax.psum_scatter(grad_down, "shard", scatter_dimension=0, tiled=True),
        lax.psum_scatter(grad_down_bias, "shard", scatter_dimension=0, tiled=True),
        lax.psum_scatter(grad_gain_two, "shard", scatter_dimension=0, tiled=True),
        lax.psum_scatter(grad_shift_two, "shard", scatter_dimension=0, tiled=True),
    )
    ffn_part = (
        lax.psum(ffn_part[0].astype(jnp.bfloat16), "rep").astype(jnp.float32),
        lax.psum(ffn_part[1].astype(jnp.bfloat16), "rep").astype(jnp.float32),
        lax.psum(ffn_part[2].astype(jnp.bfloat16), "rep").astype(jnp.float32),
        lax.psum(ffn_part[3].astype(jnp.bfloat16), "rep").astype(jnp.float32),
        lax.psum(ffn_part[4].astype(jnp.bfloat16), "rep").astype(jnp.float32),
        lax.psum(ffn_part[5].astype(jnp.bfloat16), "rep").astype(jnp.float32),
    )
    attn_back = (
        lax.all_gather(w_qkv, "shard", axis=0, tiled=True),
        lax.all_gather(b_query, "shard", axis=0, tiled=True),
        lax.all_gather(b_value, "shard", axis=0, tiled=True),
        lax.all_gather(w_out, "shard", axis=0, tiled=True),
        lax.all_gather(b_out, "shard", axis=0, tiled=True),
        lax.all_gather(ln1_gain, "shard", axis=0, tiled=True),
        lax.all_gather(ln1_bias, "shard", axis=0, tiled=True),
    )
    qkv_weight, query_bias, value_bias, out_weight, out_bias, gain_one, shift_one = attn_back
    grad_one, grad_gain_one, grad_shift_one = norm_one_pull(grad_normed)
    grad_branch = grad_one.astype(jnp.bfloat16)
    grad_out_bias = jnp.sum(grad_branch.astype(jnp.float32), axis=0)
    grad_out = inner_rows(mixed_low, grad_branch)
    grad_mixed = times_back(grad_branch, out_weight).astype(jnp.bfloat16)
    grad_qkv = lax.map(
        attend_back, (qkv_seqs, grad_mixed.reshape(seq_count, seq_len, width), log_total, valid)
    )
    grad_qkv = grad_qkv.reshape(total_rows, 3 * width)
    grad_query_bias = jnp.sum(grad_qkv[:, :width].astype(jnp.float32), axis=0)
    grad_value_bias = jnp.sum(grad_qkv[:, 2 * width :].astype(jnp.float32), axis=0)
    grad_qkv_weight = inner_rows(x_rows, grad_qkv)
    input_grad = (grad_one + times_back(grad_qkv, qkv_weight)).reshape(seq_count, seq_len, width)
    attn_part = (
        lax.psum_scatter(grad_qkv_weight, "shard", scatter_dimension=0, tiled=True),
        lax.psum_scatter(grad_query_bias, "shard", scatter_dimension=0, tiled=True),
        lax.psum_scatter(grad_value_bias, "shard", scatter_dimension=0, tiled=True),
        lax.psum_scatter(grad_out, "shard", scatter_dimension=0, tiled=True),
        lax.psum_scatter(grad_out_bias, "shard", scatter_dimension=0, tiled=True),
        lax.psum_scatter(grad_gain_one, "shard", scatter_dimension=0, tiled=True),
        lax.psum_scatter(grad_shift_one, "shard", scatter_dimension=0, tiled=True),
    )
    attn_part = (
        lax.psum(attn_part[0].astype(jnp.bfloat16), "rep").astype(jnp.float32),
        lax.psum(attn_part[1].astype(jnp.bfloat16), "rep").astype(jnp.float32),
        lax.psum(attn_part[2].astype(jnp.bfloat16), "rep").astype(jnp.float32),
        lax.psum(attn_part[3].astype(jnp.bfloat16), "rep").astype(jnp.float32),
        lax.psum(attn_part[4].astype(jnp.bfloat16), "rep").astype(jnp.float32),
        lax.psum(attn_part[5].astype(jnp.bfloat16), "rep").astype(jnp.float32),
        lax.psum(attn_part[6].astype(jnp.bfloat16), "rep").astype(jnp.float32),
    )
    return (
        layer_out,
        input_grad,
        attn_part[0],
        attn_part[1],
        attn_part[2],
        attn_part[3],
        attn_part[4],
        attn_part[5],
        attn_part[6],
        ffn_part[0],
        ffn_part[1],
        ffn_part[2],
        ffn_part[3],
        ffn_part[4],
        ffn_part[5],
    )


def solution(mesh):
    in_specs = (
        P(("shard", "rep"), None, None),
        P(("shard", "rep")),
        P("shard", None),
        P("shard"),
        P("shard"),
        P("shard", None),
        P("shard"),
        P("shard"),
        P("shard"),
        P("shard", None),
        P("shard"),
        P("shard", None),
        P("shard"),
        P("shard"),
        P("shard"),
        P(("shard", "rep"), None, None),
    )
    out_specs = (
        P(("shard", "rep"), None, None),
        P(("shard", "rep"), None, None),
        P("shard", None),
        P("shard"),
        P("shard"),
        P("shard", None),
        P("shard"),
        P("shard"),
        P("shard"),
        P("shard", None),
        P("shard"),
        P("shard", None),
        P("shard"),
        P("shard"),
        P("shard"),
    )
    return jax.shard_map(local, mesh=mesh, in_specs=in_specs, out_specs=out_specs, check_vma=False)
```

profile of v0, /device:TPU:0, one launch (start us, length us, event | category | flops | bytes accessed | tf_op | source)
XLA Modules:
  0.0 962.6 jit_solution(2393751891811151009)
XLA Ops:
  18.8 39.8 %all-reduce.18 = (bf16[768]{0:T(1024)(128)(2,1)S(1)}, bf16[768]{0:T(1024)(128)(2,1)S(1)}, bf16[768]{0:T(1024)(128)(2,1)S(1)}, bf16[768]{0:T(1024)(128)(2,1)S(1)}...) all-reduce(bf16[768]{0:T(1024)(128)(2,1)S(1)} %dynamic-update-slice, ...), channel_id=1, replica_groups=mesh['shard'=8,'rep'=4] {'shard'}, use_global_device_ids=true, to_apply=%add.1 | all-reduce | flops 6144 | bytes 24576
  61.2 25.9 %all-gather = bf16[8,1,384]{2,1,0:T(2,128)(2,1)S(1)} all-gather(bf16[1,1,384]{2,1,0:T(2,128)(2,1)S(1)} %reshape.225), channel_id=1, replica_groups=mesh['shard'=8,'rep'=4] {'shard'}, dimensions={0}, use_global_device_ids=true | all-gather | bytes 6912 | tf_op jit(solution)/shard_map/all_gather | solution.py:121
  89.6 1.7 copy.59
  91.3 2.2 copy.60
  94.1 8.4 add_convert_fusion.1
  102.5 6.7 copy.57
  109.2 24.3 %while.22 = (s32[]{:T(128)}, bf16[2,512,768]{2,1,0:T(8,128)(2,1)}, f32[2,12,512]{2,1,0:T(8,128)S(1)}, bf16[2,512,2304]{1,2,0:T(8,128)(2,1)}, pred[2,512]{1,0:T(4,128)(4,1)S(1)}, /*index=5*/s32[]{:T(128)}) while((s32[]{:T(128)}, bf16[2,512,768]{2,1,0:T(8,128)(2,1)}, f32[2,12,512]{2,1,0:T(8,128)S(1)}, bf16[2,512,2304]{1,2,0:T(8,128)(2,1)}, ...), condition=%wide.region_3.4_spmd, body=%wide.region_0.3_spmd.sunk | while | flops 843048960 | bytes 48999504 | solution.py:144
  109.4 1.8 constant_dynamic-slice_fusion.6
  111.3 3.1 fusion.82
  114.3 2.6 fusion.83
  117.0 3.3 fusion.84
  121.5 1.8 constant_dynamic-slice_fusion.6
  123.3 3.1 fusion.82
  126.4 2.6 fusion.83
  129.0 3.3 fusion.84
  134.2 3.8 fusion.40
  138.5 63.0 %all-gather.10.cloned.1.call-done = bf16[768,3072]{1,0:T(8,128)(2,1)} async-done(((bf16[96,3072]{1,0:T(8,128)(2,1)}), bf16[768,3072]{1,0:T(8,128)(2,1)}) %all-gather.10.cloned.1.call-update) | async-done | bytes 4718608 | tf_op jit(solution)/shard_map/all_gather | solution.py:120
  201.6 36.3 %multiply_convert_fusion.3 = (bf16[1024,3072]{1,0:T(8,128)(2,1)}, f32[1024,3072]{1,0:T(8,128)}, f32[1024,3072]{1,0:T(8,128)}) fusion(f32[3072]{0:T(1024)S(1)} %bitcast.162, bf16[768,3072]{1,0:T(8,128)(2,1)} %all-gather.10.cloned.1.call-done, f32[1024,768]{1,0:T(8,128)S(1)} %get-tuple-element.233, f32[768]{0:T(1024)S(1)} %copy-done.20, ...), kind=kOutput, calls=%fused_computation.45 | convolution fusion | flops 5043388416 | bytes 39348224 | tf_op jit(solution)/shard_map/dot_general | solution.py:157
  237.8 43.8 %all-gather.12.cloned.1.call-done = bf16[3072,768]{1,0:T(8,128)(2,1)} async-done(((bf16[384,768]{1,0:T(8,128)(2,1)}), bf16[3072,768]{1,0:T(8,128)(2,1)}) %all-gather.12.cloned.1.call-update) | async-done | bytes 4718608 | tf_op jit(solution)/shard_map/all_gather | solution.py:122
  281.7 8.8 fusion.41
  292.4 2.3 multiply_reduce_fusion.1
  294.7 3.1 fusion.37
  297.8 2.1 convert_reduce_fusion.1
  299.8 19.0 %convert_reduce_fusion = (f32[3072]{0:T(1024)}, bf16[1024,3072]{1,0:T(8,128)(2,1)}) fusion(f32[1024,3072]{1,0:T(8,128)} %get-tuple-element.224, bf16[1024,768]{1,0:T(8,128)(2,1)} %get-tuple-element.216, bf16[3072,768]{1,0:T(8,128)(2,1)} %all-gather.12.cloned.1.call-done, f32[1024,3072]{1,0:T(8,128)} %get-tuple-element.234, f32[3072]{0:T(1024)S(1)} %bitcast.163), kind=kOutput, calls=%fused_computation.43 | convolution fusion | flops 4885312512 | bytes 37773312 | tf_op jit(solution)/shard_map/dot_general | solution.py:29
  318.8 10.1 %multiply_reduce_fusion.2 = (f32[768]{0:T(1024)}, f32[1024]{0:T(1024)S(1)}, f32[768]{0:T(1024)}, f32[1024,768]{1,0:T(8,128)S(1)}) fusion(f32[1024,768]{1,0:T(8,128)S(1)} %get-tuple-element.233, f32[1024]{0:T(1024)S(1)} %fusion.30, f32[1024]{0:T(1024)S(1)} %broadcast_multiply_fusion.1, f32[768]{0:T(1024)S(1)} %copy-done.18, ...), kind=kOutput, calls=%fused_computation.67 | convolution fusion | flops 4839699456 | bytes 20472832 | tf_op jit(solution)/shard_map/dot_general | solution.py:29
  330.5 1.6 copy-done.5
  333.1 2.9 fusion.42
  336.0 2.6 convolution_convert_fusion
  338.6 77.7 %while.23 = (s32[]{:T(128)}, bf16[2,512,2304]{1,2,0:T(8,128)(2,1)}, bf16[2,512,2304]{1,2,0:T(8,128)(2,1)}, pred[2,512]{1,0:T(4,128)(4,1)S(1)}, f32[2,12,512]{2,1...) while((s32[]{:T(128)}, bf16[2,512,2304]{1,2,0:T(8,128)(2,1)}, bf16[2,512,2304]{1,2,0:T(8,128)(2,1)}, ...), condition=%wide.region_14.15_spmd, body=%wide.region_12.14_spmd.sunk | while | flops 2064771072 | bytes 163761360 | solution.py:220
  338.8 1.8 constant_dynamic-slice_fusion.8
  340.6 6.4 fusion.90
  349.5 11.5 %multiply_reduce_fusion.8 = (f32[12,512]{1,0:T(8,128)S(1)}, f32[12,512,512]{1,2,0:T(8,128)}) fusion(f32[12,512,512]{1,2,0:T(8,128)} %fusion.90, f32[12,512]{1,0:T(8,128)S(1)} %dynamic-slice_bitcast_fusion.2, pred[512]{0:T(512)(128)(4,1)S(1)} %dynamic-slice_reduce_fusion.5, bf16[512,12,64]{0,2,1:T(8,128)(2,1)S(1)} %bitcast.154, ...), kind=kOutput, calls=%fused_computation.17.clone.1 | convolution fusion | flops 418375680 | bytes 26796544 | tf_op jit(solution)/shard_map/while/body/eval_jaxpr/qhd,khd->hqk/dot_general | solution.py:75
  362.3 7.2 multiply_convert_fusion.5
  370.7 2.0 fusion.92
  372.7 3.1 fusion.91
  376.0 1.5 constant_dynamic-update-slice_fusion.5
  377.5 1.8 constant_dynamic-slice_fusion.8
  379.4 6.4 fusion.90
  388.2 11.5 %multiply_reduce_fusion.8 = (f32[12,512]{1,0:T(8,128)S(1)}, f32[12,512,512]{1,2,0:T(8,128)}) fusion(f32[12,512,512]{1,2,0:T(8,128)} %fusion.90, f32[12,512]{1,0:T(8,128)S(1)} %dynamic-slice_bitcast_fusion.2, pred[512]{0:T(512)(128)(4,1)S(1)} %dynamic-slice_reduce_fusion.5, bf16[512,12,64]{0,2,1:T(8,128)(2,1)S(1)} %bitcast.154, ...), kind=kOutput, calls=%fused_computation.17.clone.1 | convolution fusion | flops 418375680 | bytes 26796544 | tf_op jit(solution)/shard_map/while/body/eval_jaxpr/qhd,khd->hqk/dot_general | solution.py:75
  400.9 7.1 multiply_convert_fusion.5
  409.1 2.0 fusion.92
  411.2 3.1 fusion.91
  414.5 1.6 constant_dynamic-update-slice_fusion.5
  416.3 9.6 convolution_bitcast_fusion
  425.9 8.0 copy.69
  435.4 10.2 %fusion.43 = f32[3072,768]{1,0:T(8,128)} fusion(bf16[1024,3072]{1,0:T(8,128)(2,1)} %get-tuple-element.223, bf16[1024,768]{1,0:T(8,128)(2,1)S(1)} %copy-done.8), kind=kOutput, calls=%fused_computation.115 | convolution fusion | flops 4831838208 | bytes 17301504 | tf_op jit(solution)/shard_map/dot_general | solution.py:23
  445.7 1.8 copy-done.1
  447.5 10.7 %fusion.32 = f32[768,3072]{1,0:T(8,128)} fusion(bf16[1024,3072]{1,0:T(8,128)(2,1)} %get-tuple-element.239, f32[1024,768]{1,0:T(8,128)S(1)} %copy-done.1, f32[768]{0:T(1024)S(1)} %copy-done.21, f32[768]{0:T(1024)S(1)} %copy-done.19, f32[1024]{0:T(1024)S(1)} %copy-done.16, f32[1024]{0:T(1024)S(1)} %copy-done.14), kind=kOutput, calls=%fused_computation.107 | convolution fusion | flops 4835770368 | bytes 18888704 | tf_op jit(solution)/shard_map/dot_general | solution.py:23
  460.1 6.8 copy.63
  466.9 2.7 convert_reduce_fusion.3
  469.6 37.0 %all-reduce.17 = (bf16[768]{0:T(1024)(128)(2,1)S(1)}, bf16[768]{0:T(1024)(128)(2,1)S(1)}, bf16[768]{0:T(1024)(128)(2,1)S(1)}, bf16[768]{0:T(1024)(128)(2,1)S(1)}...) all-reduce(f32[768]{0:T(1024)S(1)} %get-tuple-element.161, ...), channel_id=3, replica_groups=mesh['shard'=8,'rep'=4] {'shard'}, use_global_device_ids=true, to_apply=%region_18.19.clone | all-reduce | flops 9216 | bytes 55296
  507.3 6.0 all-reduce.19
  518.0 1.6 convert_element_type.212
  519.7 43.1 %reduce-scatter.13.cloned.1.call-done = f32[96,2304]{1,0:T(8,128)} async-done(((f32[768,2304]{1,0:T(8,128)}), f32[96,2304]{1,0:T(8,128)}) %reduce-scatter.13.cloned.1.call-update) | async-done | bytes 884752
  562.8 2.2 copy.70
  565.0 164.3 %reduce-scatter.11.cloned.1.call-done = f32[384,768]{1,0:T(8,128)} async-done(((f32[3072,768]{1,0:T(8,128)}), f32[384,768]{1,0:T(8,128)}) %reduce-scatter.11.cloned.1.call-update) | async-done | bytes 1179664 | tf_op jit(solution)/shard_map/reduce_scatter | solution.py:192
  729.3 2.1 convert_element_type.226
  731.5 164.5 %reduce-scatter.9.cloned.1.call-done = f32[96,3072]{1,0:T(8,128)} async-done(((f32[768,3072]{1,0:T(8,128)}), f32[96,3072]{1,0:T(8,128)}) %reduce-scatter.9.cloned.1.call-update) | async-done | bytes 1179664 | tf_op jit(solution)/shard_map/reduce_scatter | solution.py:190
  896.0 2.2 convert_element_type.221
  898.2 9.0 add_add_fusion.4
  907.1 41.1 %all-reduce.23.cloned.1.call-done = (bf16[96,2304]{0,1:T(8,128)(2,1)}, bf16[96,768]{1,0:T(8,128)(2,1)}, bf16[96,3072]{1,0:T(8,128)(2,1)}, bf16[384,768]{1,0:T(8,128)(2,1)}) async-done(((bf16[96,2304]{0,1:T(8,128)(2,1)}, bf16[96,768]{1,0:T(8,128)(2,1)}, bf16[96,3072]{1,0:T(8,128)(2,1)}, bf16[384,768]{1,0:T(8,128)(2,1)}), (bf16[96,2304]{0,1:T(8,128)(2,1)}, bf16[96,768]{1,0:T(8,128)(2,1)}, ...) | async-done | bytes 1769488 | tf_op jit(solution)/shard_map/psum | solution.py:238
  948.2 2.2 convert_element_type.222
  950.5 2.2 convert_element_type.227
  952.6 2.2 copy.64
  (195 shorter events, 42.6 us)
Async XLA Ops:
  7.2 86.9 %all-gather.6.cloned.1.call-start = ((), (), s32[]{:S(2)}) async-start(), calls=%async_computation.4 | async-start | bytes 3981312 | tf_op jit(solution)/shard_map/all_gather | solution.py:111
  7.9 125.6 %all-gather.8.cloned.1.call-start = ((), (), s32[]{:S(2)}) async-start(), calls=%async_computation.5 | async-start | bytes 1327104 | tf_op jit(solution)/shard_map/all_gather | solution.py:114
  8.7 192.9 %all-gather.10.cloned.1.call-start = ((), (), s32[]{:S(2)}) async-start(), calls=%async_computation.6 | async-start | bytes 5308416 | tf_op jit(solution)/shard_map/all_gather | solution.py:120
  9.4 272.3 %all-gather.12.cloned.1.call-start = ((), (), s32[]{:S(2)}) async-start(), calls=%async_computation.7 | async-start | bytes 5308416 | tf_op jit(solution)/shard_map/all_gather | solution.py:122
  10.0 508.1 %reduce-scatter.7.cloned.1.call-start = ((), (), s32[]{:S(2)}) async-start(), calls=%async_computation.8 | async-start | bytes 2654208 | tf_op jit(solution)/shard_map/reduce_scatter | solution.py:232
  91.3 11.2 %copy-start.3 = (bf16[2,512,768]{1,2,0:T(8,128)(2,1)}, bf16[2,512,768]{1,2,0:T(8,128)(2,1)S(1)}, u32[]{:S(2)}) copy-start(bf16[2,512,768]{1,2,0:T(8,128)(2,1)S(1)} %copy.59) | copy-start | bytes 4718596
  133.5 0.6 copy-start.9
  133.5 0.6 copy-start.11
  134.2 67.4 %copy-start.18 = (f32[768]{0:T(1024)S(1)}, f32[768]{0:T(1024)}, u32[]{:S(2)}) copy-start(f32[768]{0:T(1024)} %convert_element_type.189) | copy-start | bytes 9220
  134.2 67.4 %copy-start.20 = (f32[768]{0:T(1024)S(1)}, f32[768]{0:T(1024)}, u32[]{:S(2)}) copy-start(f32[768]{0:T(1024)} %convert_element_type.190) | copy-start | bytes 9220
  134.2 67.4 %copy-start.29 = (f32[8,1,384]{2,1,0:T(1,128)S(1)}, f32[8,1,384]{2,1,0:T(1,128)}, u32[]{:S(2)}) copy-start(f32[8,1,384]{2,1,0:T(1,128)} %convert_element_type.237) | copy-start | bytes 36868
  138.0 191.0 %copy-start = (f32[1024,768]{1,0:T(8,128)}, f32[1024,768]{1,0:T(8,128)S(1)}, u32[]{:S(2)}) copy-start(f32[1024,768]{1,0:T(8,128)S(1)} %get-tuple-element.233) | copy-start | bytes 9437188
  138.0 191.0 %copy-start.13 = (f32[1024]{0:T(1024)}, f32[1024]{0:T(1024)S(1)}, u32[]{:S(2)}) copy-start(f32[1024]{0:T(1024)S(1)} %broadcast_multiply_fusion.1) | copy-start | bytes 12292
  138.5 190.5 %copy-start.15 = (f32[1024]{0:T(1024)}, f32[1024]{0:T(1024)S(1)}, u32[]{:S(2)}) copy-start(f32[1024]{0:T(1024)S(1)} %fusion.30) | copy-start | bytes 12292
  201.6 80.1 %copy-start.32 = (f32[768]{0:T(1024)S(1)}, f32[768]{0:T(1024)}, u32[]{:S(2)}) copy-start(f32[768]{0:T(1024)} %convert_element_type.194) | copy-start | bytes 9220
  281.7 9.4 copy-start.22
  281.7 9.4 copy-start.31
  290.5 1.9 copy-start.2
  290.5 4.2 copy-start.23
  330.5 1.7 copy-start.5
  330.5 2.6 copy-start.35
  330.5 2.6 copy-start.24
  333.1 3.0 copy-start.36
  336.0 2.7 copy-start.10
  336.0 2.6 copy-start.12
  336.0 226.8 %reduce-scatter.13.cloned.1.call-start = ((), (), s32[]{:S(2)}) async-start(), calls=%async_computation.11 | async-start | bytes 7962624
  340.6 6.4 copy-start.7
  349.4 11.6 %slice-start = ((s8[12582912]{0:T(1024)(128)(4,1)}), s8[4194304]{0:T(1024)(128)(4,1)S(1)}, s32[]{:S(2)}) async-start(s8[12582912]{0:T(1024)(128)(4,1)} %bitcast.145), calls=%async_computation.13 | async-start | bytes 8388608 | tf_op jit(solution)/shard_map/while
  349.4 11.6 %slice-start.1 = ((s8[12582912]{0:T(1024)(128)(4,1)}), s8[4194304]{0:T(1024)(128)(4,1)S(1)}, s32[]{:S(2)}) async-start(s8[12582912]{0:T(1024)(128)(4,1)} %bitcast.145), calls=%async_computation.14 | async-start | bytes 8388608 | tf_op jit(solution)/shard_map/while
  349.4 12.9 %slice-start.2 = ((s8[12582912]{0:T(1024)(128)(4,1)}), s8[4194304]{0:T(1024)(128)(4,1)S(1)}, s32[]{:S(2)}) async-start(s8[12582912]{0:T(1024)(128)(4,1)} %bitcast.145), calls=%async_computation.15 | async-start | bytes 8388608 | tf_op jit(solution)/shard_map/while
  379.3 6.4 copy-start.7
  388.1 11.5 %slice-start = ((s8[12582912]{0:T(1024)(128)(4,1)}), s8[4194304]{0:T(1024)(128)(4,1)S(1)}, s32[]{:S(2)}) async-start(s8[12582912]{0:T(1024)(128)(4,1)} %bitcast.145), calls=%async_computation.13 | async-start | bytes 8388608 | tf_op jit(solution)/shard_map/while
  388.1 11.5 %slice-start.1 = ((s8[12582912]{0:T(1024)(128)(4,1)}), s8[4194304]{0:T(1024)(128)(4,1)S(1)}, s32[]{:S(2)}) async-start(s8[12582912]{0:T(1024)(128)(4,1)} %bitcast.145), calls=%async_computation.14 | async-start | bytes 8388608 | tf_op jit(solution)/shard_map/while
  388.2 12.7 %slice-start.2 = ((s8[12582912]{0:T(1024)(128)(4,1)}), s8[4194304]{0:T(1024)(128)(4,1)S(1)}, s32[]{:S(2)}) async-start(s8[12582912]{0:T(1024)(128)(4,1)} %bitcast.145), calls=%async_computation.15 | async-start | bytes 8388608 | tf_op jit(solution)/shard_map/while
  433.9 1.4 copy-start.8
  434.0 295.4 %reduce-scatter.11.cloned.1.call-start = ((), (), s32[]{:S(2)}) async-start(), calls=%async_computation.10 | async-start | bytes 10616832 | tf_op jit(solution)/shard_map/reduce_scatter | solution.py:192
  445.6 1.9 copy-start.1
  445.6 1.9 copy-start.14
  445.6 1.9 copy-start.16
  445.6 1.9 copy-start.19
  445.6 1.9 copy-start.21
  445.6 450.3 %reduce-scatter.9.cloned.1.call-start = ((), (), s32[]{:S(2)}) async-start(), calls=%async_computation.9 | async-start | bytes 10616832 | tf_op jit(solution)/shard_map/reduce_scatter | solution.py:190
  458.1 1.5 copy-start.4
  458.2 490.1 %all-reduce.23.cloned.1.call-start = ((), (), s32[]{:S(2)}) async-start(), calls=%async_computation.12 | async-start | bytes 3833856 | tf_op jit(solution)/shard_map/psum | solution.py:238
  460.0 9.6 copy-start.26
  460.0 9.6 copy-start.27
  460.0 9.6 copy-start.28
  460.0 9.6 copy-start.30
  460.1 9.6 copy-start.33
  460.1 9.6 copy-start.34
  466.9 431.3 %copy-start.6 = (f32[1024,768]{1,0:T(8,128)S(1)}, f32[1024,768]{1,0:T(8,128)}, u32[]{:S(2)}) copy-start(f32[1024,768]{1,0:T(8,128)} %copy-done.5) | copy-start | bytes 9437188
  466.9 431.3 %copy-start.25 = (f32[1024]{0:T(1024)S(1)}, f32[1024]{0:T(1024)}, u32[]{:S(2)}) copy-start(f32[1024]{0:T(1024)} %copy-done.24) | copy-start | bytes 12292
  948.2 6.6 copy-start.17
Sparse Core Ops, SparseCore 0:
  10.2 68.5 all-gather.5
  80.9 39.7 all-gather.7
  122.9 78.6 all-gather.9
  203.6 78.0 all-gather.11
  336.1 67.3 reduce-scatter.6
  434.1 128.6 reduce-scatter.12
  566.8 162.5 reduce-scatter.10
  733.4 162.5 reduce-scatter.8
  899.9 48.2 all-reduce.22
where the time goes:
time: 969 us; the launch traced here: 963 us
  waiting for transfers between devices  523 us (54%)
  matrix products  192 us (20%)
  blocking collectives  109 us (11%)
  local copies, waits for them, and re-layouts  66.8 us (7%)
  other arithmetic  54.1 us (6%)
  between operations  16.9 us (2%)
    reduce_scatter x1, waiting for transfers between devices, local(): lax.psum_scatter(grad_up, 'shard', scatter_dimension=0, tiled=True)  164 us
    reduce_scatter x1, waiting for transfers between devices, local(): lax.psum_scatter(grad_down, 'shard', scatter_dimension=0, tiled=True)  164 us
    unnamed x2, blocking collectives  76.8 us
    all_gather x1, waiting for transfers between devices, local(): lax.all_gather(w_up, 'shard', axis=0, tiled=True)  63 us
    unnamed x10, waiting for transfers between devices  45.8 us
    all_gather x1, waiting for transfers between devices, local(): lax.all_gather(w_down, 'shard', axis=0, tiled=True)  43.8 us
    psum x1, waiting for transfers between devices, local(): lax.psum(attn_part[0].astype(jnp.bfloat16), 'rep').astype(jnp.float32)  41.1 us
    dot_general x4, matrix products, times_back(): lax.dot_general(left, right, (((1,), (1,)), ((), ())), preferred_element_...  40.6 us
  transfers between devices with their start and end apart: 9, of which 6 were waited for; matrix products, arithmetic and copies ran while one was open for 25% of the time, Pallas kernels for 0%

commit v1 on v0

v1 whole, which is shorter than its diff:
```python
import functools

import jax
import jax.numpy as jnp
from jax import lax
from jax.experimental import pallas as pl
from jax.experimental.pallas import tpu as pltpu
from jax.sharding import PartitionSpec as P

HEADS = 12
EPS = 1e-05
F32 = jnp.float32
BF16 = jnp.bfloat16
BLOCKS = 8
VMEM_LIMIT = 58 * 1024 * 1024


def dot_nn(a, b):
    return lax.dot_general(a, b, (((1,), (0,)), ((), ())), preferred_element_type=F32)


def dot_nt(a, b):
    return lax.dot_general(a, b, (((1,), (1,)), ((), ())), preferred_element_type=F32)


def dot_tn(a, b):
    return lax.dot_general(a, b, (((0,), (0,)), ((), ())), preferred_element_type=F32)


def params(grid_dims):
    return pltpu.CompilerParams(
        dimension_semantics=("arbitrary",) * grid_dims, vmem_limit_bytes=VMEM_LIMIT
    )


def cost(flops, nbytes, trans=0):
    return pl.CostEstimate(flops=int(flops), bytes_accessed=int(nbytes), transcendentals=int(trans))


def turned(place):
    return ((place & 1) << 2) | (place & 2) | ((place >> 2) & 1)


def place_rows(meta, source, target, columns, cut):
    rows = source.shape[2]
    for half in range(2):
        for block in range(BLOCKS):
            start = (meta[0] ^ turned(block)) * (2 * rows) + (meta[1] ^ half) * rows
            target[pl.ds(pl.multiple_of(start, 16), rows), cut] = source[half, block, :, columns]


def attend_kernel(meta, x_ref, mine_ref, other_ref, bias_ref, qkv_ref, mixed_ref, lse_ref, w_scr):
    half, seq = pl.program_id(0), pl.program_id(1)
    wide = w_scr.shape[1]
    part = wide // 3

    @pl.when((seq == 0) & (half == 0))
    def _():
        place_rows(meta, mine_ref, w_scr, slice(None), slice(None))

    @pl.when((seq == 0) & (half == 1))
    def _():
        place_rows(meta, other_ref, w_scr, slice(None), slice(None))

    length = meta[3 + seq]
    qkv = (dot_nn(x_ref[0], w_scr[...]) + bias_ref[0]).astype(BF16)
    qkv_ref[0, 0] = qkv
    rows = qkv.shape[0]
    lane = lax.broadcasted_iota(jnp.int32, (rows, 128), 1)
    key_ok = lax.broadcasted_iota(jnp.int32, (rows, rows), 0) < length
    for pair in range(part // 128):
        cut = pair * 128
        query = qkv[:, cut : cut + 128] * jnp.asarray(0.125, BF16)
        key = qkv[:, part + cut : part + cut + 128]
        value_t = qkv[:, 2 * part + cut : 2 * part + cut + 128].T
        outs = []
        for head in range(2):
            query_one = jnp.where((lane >= 64) == (head == 1), query, jnp.zeros_like(query))
            scores = jnp.where(key_ok, dot_nt(key, query_one), -1e30)
            top = jnp.max(scores, axis=0, keepdims=True)
            exp_scores = jnp.exp(scores - top)
            total = jnp.sum(exp_scores, axis=0, keepdims=True)
            lse_ref[0, 0, 2 * pair + head] = top + jnp.log(total)
            out = dot_nn(value_t[64 * head : 64 * head + 64], exp_scores.astype(BF16))
            outs.append(out * (1.0 / total))
        mixed_ref[0, :, cut : cut + 128] = jnp.concatenate(outs, axis=0).T.astype(BF16)


def attend(meta, x, mine, other, bias):
    seqs, length, width = x.shape
    wide = mine.shape[3]
    half_heads = HEADS // 2
    whole = lambda h, s, m: (0, 0, 0, 0)
    return pl.pallas_call(
        attend_kernel,
        grid_spec=pltpu.PrefetchScalarGridSpec(
            num_scalar_prefetch=1,
            grid=(2, seqs),
            in_specs=[
                pl.BlockSpec((1, length, width), lambda h, s, m: (s, 0, 0)),
                pl.BlockSpec(mine.shape, whole, pipeline_mode=pl.Buffered(1)),
                pl.BlockSpec(other.shape, whole, pipeline_mode=pl.Buffered(1)),
                pl.BlockSpec((1, 1, wide), lambda h, s, m: (m[2] ^ h, 0, 0)),
            ],
            out_specs=[
                pl.BlockSpec((1, 1, length, wide), lambda h, s, m: (m[2] ^ h, s, 0, 0)),
                pl.BlockSpec((1, length, wide // 3), lambda h, s, m: (s, 0, m[2] ^ h)),
                pl.BlockSpec(
                    (1, 1, half_heads, 1, length), lambda h, s, m: (m[2] ^ h, s, 0, 0, 0)
                ),
            ],
            scratch_shapes=[pltpu.VMEM((width, wide), BF16)],
        ),
        out_shape=[
            jax.ShapeDtypeStruct((2, seqs, length, wide), BF16),
            jax.ShapeDtypeStruct((seqs, length, width), BF16),
            jax.ShapeDtypeStruct((2, seqs, half_heads, 1, length), F32),
        ],
        compiler_params=params(2),
        cost_estimate=cost(
            4 * seqs * length * width * wide + 4 * seqs * length * length * width * 4,
            20e6,
            seqs * length * length * HEADS,
        ),
        name="attend_forward",
    )(meta, x, mine, other, bias)


def gelu_and_slope(hidden):
    size = jnp.abs(hidden)
    bell = jnp.exp(-0.5 * hidden * hidden)
    t = 1.0 / (1.0 + (0.3275911 * 0.7071067811865476) * size)
    poly = t * (
        0.5 * 0.254829592
        + t
        * (
            0.5 * -0.284496736
            + t * (0.5 * 1.421413741 + t * (0.5 * -1.453152027 + t * (0.5 * 1.061405429)))
        )
    )
    tail = poly * bell
    phi = jnp.where(hidden < 0.0, tail, 1.0 - tail)
    return hidden * phi, phi + hidden * bell * 0.3989422804014327


def norm_forward(hidden):
    center = hidden - jnp.mean(hidden, axis=-1, keepdims=True)
    scale = lax.rsqrt(jnp.mean(center * center, axis=-1, keepdims=True) + EPS)
    return center * scale, scale


def norm_back(grad, hat, scale, gain):
    grad_hat = grad * gain
    shift = jnp.mean(grad_hat, axis=-1, keepdims=True)
    along = jnp.mean(grad_hat * hat, axis=-1, keepdims=True)
    return scale * (grad_hat - shift - hat * along)


def column_sum(rows):
    return jnp.sum(rows.astype(F32), axis=0, keepdims=True)


def feed_kernel(
    seq_len,
    meta,
    x_ref,
    mixed_ref,
    cot_ref,
    up_mine,
    up_other,
    down_mine,
    down_other,
    vec_ref,
    b_up_ref,
    out_ref,
    norm_ref,
    active_ref,
    grad_hidden_ref,
    grad_second_ref,
    grad_branch_ref,
    grad_mixed_ref,
    grad_vec_ref,
    grad_b_up_ref,
    w_up,
    w_out,
    w_down,
    slope_scr,
):
    step = pl.program_id(0)
    tile, width = x_ref.shape
    hidden_width = w_up.shape[1]
    groups = 3
    up_cut, out_cut = hidden_width // (2 * groups), width // (2 * groups)

    @pl.when(step == 0)
    def _():
        grad_vec_ref[...] = jnp.zeros_like(grad_vec_ref)
        grad_b_up_ref[...] = jnp.zeros_like(grad_b_up_ref)
        for rel, source in enumerate((up_mine, up_other)):
            core = meta[2] ^ rel
            for group in range(groups):
                base = group * (up_cut + out_cut)
                up_to = pl.multiple_of(core * (hidden_width // 2) + group * up_cut, 128)
                out_to = pl.multiple_of(core * (width // 2) + group * out_cut, 128)
                place_rows(meta, source, w_up, slice(base, base + up_cut), pl.ds(up_to, up_cut))
                place_rows(
                    meta,
                    source,
                    w_out,
                    slice(base + up_cut, base + up_cut + out_cut),
                    pl.ds(out_to, out_cut),
                )
        rows = down_mine.shape[2]
        for rel, source in enumerate((down_mine, down_other)):
            for half in range(2):
                for block in range(BLOCKS):
                    start = (
                        (meta[0] ^ turned(block)) * (4 * rows)
                        + (meta[2] ^ rel) * (2 * rows)
                        + (meta[1] ^ half) * rows
                    )
                    w_down[pl.ds(pl.multiple_of(start, 16), rows), :] = source[half, block]

    vec = vec_ref[...]
    b_out, gain_one, shift_one, b_down, gain_two, shift_two = [vec[i : i + 1] for i in range(6)]
    seq = lax.div(step * tile, seq_len)
    place = lax.broadcasted_iota(jnp.int32, (tile, 1), 0) + lax.rem(step * tile, seq_len)
    valid = place < meta[3 + seq]

    hat_one, scale_one = norm_forward(
        x_ref[...].astype(F32) + (dot_nn(mixed_ref[...], w_out[...]) + b_out)
    )
    normed = hat_one * gain_one + shift_one
    normed_low = normed.astype(BF16)
    norm_ref[...] = normed_low
    chunk = 512
    second = jnp.zeros((tile, width), F32)
    for start in range(0, hidden_width, chunk):
        cut = slice(start, start + chunk)
        hidden = dot_nn(normed_low, w_up[:, cut]) + b_up_ref[:, cut]
        active, slope = gelu_and_slope(hidden)
        slope_scr[:, cut] = slope
        active_low = active.astype(BF16)
        active_ref[:, cut] = active_low
        second = second + dot_nn(active_low, w_down[cut, :])
    hat_two, scale_two = norm_forward(normed + (second + b_down))
    out_ref[...] = jnp.where(valid, hat_two * gain_two + shift_two, 0.0).astype(BF16)

    grad_result = jnp.where(valid, cot_ref[...].astype(F32), 0.0)
    grad_two = norm_back(grad_result, hat_two, scale_two, gain_two)
    grad_second = grad_two.astype(BF16)
    grad_second_ref[...] = grad_second
    grad_normed = grad_two
    for start in range(0, hidden_width, chunk):
        cut = slice(start, start + chunk)
        grad_active = dot_nt(grad_second, w_down[cut, :])
        grad_hidden = (slope_scr[:, cut] * grad_active).astype(BF16)
        grad_hidden_ref[:, cut] = grad_hidden
        grad_b_up_ref[:, cut] += column_sum(grad_hidden)
        grad_normed = grad_normed + dot_nt(grad_hidden, w_up[:, cut])
    grad_one = norm_back(grad_normed, hat_one, scale_one, gain_one)
    grad_branch = grad_one.astype(BF16)
    grad_branch_ref[...] = grad_branch
    grad_mixed_ref[...] = dot_nt(grad_branch, w_out[...]).astype(BF16)
    sums = (
        column_sum(grad_branch),
        column_sum(grad_normed * hat_one),
        column_sum(grad_normed),
        column_sum(grad_second),
        column_sum(grad_result * hat_two),
        column_sum(grad_result),
    )
    for i, total in enumerate(sums):
        grad_vec_ref[i : i + 1, :] += total


def feed(meta, x, mixed, cot, up, down, vec, b_up, seq_len):
    rows, width = x.shape
    hidden_width = b_up.shape[1]
    tile = min(256, rows)
    by_row = lambda cols: pl.BlockSpec((tile, cols), lambda i, m: (i, 0))
    whole = lambda a: pl.BlockSpec(
        a.shape, lambda i, m: (0,) * a.ndim, pipeline_mode=pl.Buffered(1)
    )
    rows_of = lambda cols: jax.ShapeDtypeStruct((rows, cols), BF16)
    return pl.pallas_call(
        functools.partial(feed_kernel, seq_len),
        grid_spec=pltpu.PrefetchScalarGridSpec(
            num_scalar_prefetch=1,
            grid=(rows // tile,),
            in_specs=[by_row(width)] * 3 + [whole(a) for a in (*up, *down, vec, b_up)],
            out_specs=[
                by_row(width),
                by_row(width),
                by_row(hidden_width),
                by_row(hidden_width),
                by_row(width),
                by_row(width),
                by_row(width),
                pl.BlockSpec((8, width), lambda i, m: (0, 0)),
                pl.BlockSpec((1, hidden_width), lambda i, m: (0, 0)),
            ],
            scratch_shapes=[
                pltpu.VMEM((width, hidden_width), BF16),
                pltpu.VMEM((width, width), BF16),
                pltpu.VMEM((hidden_width, width), BF16),
                pltpu.VMEM((tile, hidden_width), F32),
            ],
        ),
        out_shape=[
            rows_of(width),
            rows_of(width),
            rows_of(hidden_width),
            rows_of(hidden_width),
            rows_of(width),
            rows_of(width),
            rows_of(width),
            jax.ShapeDtypeStruct((8, width), F32),
            jax.ShapeDtypeStruct((1, hidden_width), F32),
        ],
        compiler_params=params(1),
        cost_estimate=cost(
            8 * rows * width * hidden_width + 4 * rows * width * width,
            40e6,
            2 * rows * hidden_width,
        ),
        name="feed_forward_and_back",
    )(meta, x, mixed, cot, *up, *down, vec, b_up)


def store_blocks(meta, out_ref, value, cut):
    rows = out_ref.shape[2]
    for block in range(BLOCKS):
        for half in range(2):
            start = (2 * block + half) * rows
            out_ref[meta[1] ^ half, turned(meta[0] ^ block), :, cut] = value[
                start : start + rows
            ].astype(BF16)


def grad_up_kernel(meta, norm_ref, mixed_ref, grad_hidden_ref, grad_branch_ref, out_ref):
    up_cut = grad_hidden_ref.shape[1]
    store_blocks(meta, out_ref, dot_tn(norm_ref[...], grad_hidden_ref[...]), slice(0, up_cut))
    store_blocks(
        meta,
        out_ref,
        dot_tn(mixed_ref[...], grad_branch_ref[...]),
        slice(up_cut, out_ref.shape[3]),
    )


def grad_up(rel, meta, normed, mixed, grad_hidden, grad_branch):
    rows, width = normed.shape
    hidden_width = grad_hidden.shape[1]
    groups = 3
    up_cut, out_cut = hidden_width // (2 * groups), width // (2 * groups)
    block_rows = width // (2 * BLOCKS)
    whole = pl.BlockSpec((rows, width), lambda n, m: (0, 0), pipeline_mode=pl.Buffered(1))
    turn = lambda n, m: (0, (m[2] ^ rel) * groups + n)
    return pl.pallas_call(
        grad_up_kernel,
        grid_spec=pltpu.PrefetchScalarGridSpec(
            num_scalar_prefetch=1,
            grid=(groups,),
            in_specs=[
                whole,
                whole,
                pl.BlockSpec((rows, up_cut), turn),
                pl.BlockSpec((rows, out_cut), turn),
            ],
            out_specs=pl.BlockSpec(
                (2, BLOCKS, block_rows, up_cut + out_cut), lambda n, m: (0, 0, 0, n)
            ),
        ),
        out_shape=jax.ShapeDtypeStruct(
            (2, BLOCKS, block_rows, groups * (up_cut + out_cut)), BF16
        ),
        compiler_params=params(1),
        cost_estimate=cost(rows * width * (hidden_width + width), 12e6),
        name="grad_up",
    )(meta, normed, mixed, grad_hidden, grad_branch)


def grad_down_kernel(meta, active_ref, grad_second_ref, keep_ref, send_ref):
    value = dot_tn(active_ref[...], grad_second_ref[...])
    rows = keep_ref.shape[2]
    mine = meta[2] == 0
    low, high = value[: 2 * rows], value[2 * rows :]
    keep = jnp.where(mine, low, high).astype(BF16)
    send = jnp.where(mine, high, low).astype(BF16)
    for half in range(2):
        keep_ref[meta[1] ^ half, 0] = keep[half * rows : (half + 1) * rows]
        send_ref[meta[1] ^ half, 0] = send[half * rows : (half + 1) * rows]


def grad_down(meta, active, grad_second):
    rows, hidden_width = active.shape
    width = grad_second.shape[1]
    block = hidden_width // BLOCKS
    out = jax.ShapeDtypeStruct((2, BLOCKS, block // 4, width), BF16)
    spec = pl.BlockSpec((2, 1, block // 4, width), lambda j, m: (0, j, 0, 0))
    return pl.pallas_call(
        grad_down_kernel,
        grid_spec=pltpu.PrefetchScalarGridSpec(
            num_scalar_prefetch=1,
            grid=(BLOCKS,),
            in_specs=[
                pl.BlockSpec((rows, block), lambda j, m: (0, m[0] ^ turned(j))),
                pl.BlockSpec((rows, width), lambda j, m: (0, 0), pipeline_mode=pl.Buffered(1)),
            ],
            out_specs=[spec, spec],
        ),
        out_shape=[out, out],
        compiler_params=params(1),
        cost_estimate=cost(2 * rows * hidden_width * width, 16e6),
        name="grad_down",
    )(meta, active, grad_second)


def attend_back_kernel(
    meta,
    x_ref,
    qkv_ref,
    mixed_ref,
    grad_mixed_ref,
    lse_ref,
    grad_qkv_ref,
    grad_w_ref,
    grad_bias_ref,
    grad_scr,
):
    seq = pl.program_id(0)
    length = meta[3 + seq]
    rows, wide = qkv_ref.shape[2:]
    part = wide // 3
    lane = lax.broadcasted_iota(jnp.int32, (rows, 128), 1)
    key_ok = lax.broadcasted_iota(jnp.int32, (rows, rows), 0) < length

    @pl.when(seq == 0)
    def _():
        grad_bias_ref[...] = jnp.zeros_like(grad_bias_ref)

    grads = [[], [], []]
    for pair in range(part // 128):
        cut = pair * 128
        query = qkv_ref[0, 0, :, cut : cut + 128] * jnp.asarray(0.125, BF16)
        key = qkv_ref[0, 0, :, part + cut : part + cut + 128]
        value = qkv_ref[0, 0, :, 2 * part + cut : 2 * part + cut + 128]
        grad_out = grad_mixed_ref[0, :, cut : cut + 128]
        product = (grad_out.astype(F32) * mixed_ref[0, :, cut : cut + 128].astype(F32)).T
        key_t = key.T
        grad_query, grad_key, grad_value = [], 0.0, 0.0
        for head in range(2):
            keep = (lane >= 64) == (head == 1)
            query_one = jnp.where(keep, query, jnp.zeros_like(query))
            grad_one = jnp.where(keep, grad_out, jnp.zeros_like(grad_out))
            inner = slice(64 * head, 64 * head + 64)
            delta = jnp.sum(product[inner], axis=0, keepdims=True)
            log_total = lse_ref[0, 0, 2 * pair + head]
            scores = jnp.where(key_ok, dot_nt(key, query_one), -1e30)
            prob = jnp.exp(scores - log_total)
            grad_prob = dot_nt(value, grad_one)
            grad_scores = (prob * (grad_prob - delta)).astype(BF16)
            grad_value = grad_value + dot_nn(prob.astype(BF16), grad_one)
            grad_key = grad_key + dot_nn(grad_scores, query_one)
            grad_query.append(dot_nn(key_t[inner], grad_scores) * 0.125)
        grads[0].append(jnp.concatenate(grad_query, axis=0).T.astype(BF16))
        grads[1].append(grad_key.astype(BF16))
        grads[2].append(grad_value.astype(BF16))
    start = pl.multiple_of(seq * rows, 128)
    for kind in range(3):
        for pair, grad in enumerate(grads[kind]):
            cut = slice(kind * part + pair * 128, kind * part + (pair + 1) * 128)
            grad_scr[pl.ds(start, rows), cut] = grad
            grad_qkv_ref[0, :, cut] = grad
            grad_bias_ref[:, cut] += column_sum(grad)

    @pl.when(seq == pl.num_programs(0) - 1)
    def _():
        store_blocks(meta, grad_w_ref, dot_tn(x_ref[...], grad_scr[...]), slice(None))


def attend_back(rel, meta, x, qkv, mixed, grad_mixed, lse):
    _, seqs, length, wide = qkv.shape
    width = mixed.shape[2]
    rows = seqs * length
    half_heads = HEADS // 2
    block_rows = width // (2 * BLOCKS)
    by_half = pl.BlockSpec((1, length, wide // 3), lambda s, m: (s, 0, m[2] ^ rel))
    return pl.pallas_call(
        attend_back_kernel,
        grid_spec=pltpu.PrefetchScalarGridSpec(
            num_scalar_prefetch=1,
            grid=(seqs,),
            in_specs=[
                pl.BlockSpec((rows, width), lambda s, m: (0, 0), pipeline_mode=pl.Buffered(1)),
                pl.BlockSpec((1, 1, length, wide), lambda s, m: (m[2] ^ rel, s, 0, 0)),
                by_half,
                by_half,
                pl.BlockSpec(
                    (1, 1, half_heads, 1, length), lambda s, m: (m[2] ^ rel, s, 0, 0, 0)
                ),
            ],
            out_specs=[
                pl.BlockSpec((1, length, wide), lambda s, m: (s, 0, 0)),
                pl.BlockSpec((2, BLOCKS, block_rows, wide), lambda s, m: (0, 0, 0, 0)),
                pl.BlockSpec((1, wide), lambda s, m: (0, 0)),
            ],
            scratch_shapes=[pltpu.VMEM((rows, wide), BF16)],
        ),
        out_shape=[
            jax.ShapeDtypeStruct((seqs, length, wide), BF16),
            jax.ShapeDtypeStruct((2, BLOCKS, block_rows, wide), BF16),
            jax.ShapeDtypeStruct((1, wide), F32),
        ],
        compiler_params=params(1),
        cost_estimate=cost(
            2 * rows * width * wide + 5 * rows * length * width * 4,
            16e6,
            rows * length * half_heads,
        ),
        name="attend_back",
    )(meta, x.reshape(rows, width), qkv, mixed, grad_mixed, lse)


def input_kernel(meta, branch_ref, mine_ref, other_ref, w_mine, w_other, out_ref, scr_mine, scr_other):
    @pl.when(pl.program_id(0) == 0)
    def _():
        place_rows(meta, w_mine, scr_mine, slice(None), slice(None))
        place_rows(meta, w_other, scr_other, slice(None), slice(None))

    out_ref[...] = (
        branch_ref[...].astype(F32)
        + dot_nt(mine_ref[...], scr_mine[...])
        + dot_nt(other_ref[...], scr_other[...])
    )


def input_grad_of(meta, grad_branch, grad_mine, grad_other, w_mine, w_other):
    rows, width = grad_branch.shape
    wide = grad_mine.shape[1]
    tile = min(256, rows)
    whole = pl.BlockSpec(w_mine.shape, lambda i, m: (0, 0, 0, 0), pipeline_mode=pl.Buffered(1))
    by_row = lambda cols: pl.BlockSpec((tile, cols), lambda i, m: (i, 0))
    return pl.pallas_call(
        input_kernel,
        grid_spec=pltpu.PrefetchScalarGridSpec(
            num_scalar_prefetch=1,
            grid=(rows // tile,),
            in_specs=[by_row(width), by_row(wide), by_row(wide), whole, whole],
            out_specs=by_row(width),
            scratch_shapes=[pltpu.VMEM((width, wide), BF16)] * 2,
        ),
        out_shape=jax.ShapeDtypeStruct((rows, width), F32),
        compiler_params=params(1),
        cost_estimate=cost(4 * rows * width * wide, 14e6),
        name="input_grad",
    )(meta, grad_branch, grad_mine, grad_other, w_mine, w_other)


def swap(array, axis, size, bit):
    return lax.ppermute(array, axis, [(i, i ^ bit) for i in range(size)])


def gather_quarters(piece):
    held = piece[None]
    for bit in (4, 2, 1):
        came = swap(held, "shard", BLOCKS, bit)
        held = jnp.concatenate([held, came], axis=0)
    came = swap(held, "rep", 4, 2)
    mine = jnp.stack([held, came])
    return mine, swap(mine, "rep", 4, 1)


def add(left, right):
    return (left.astype(F32) + right.astype(F32)).astype(BF16)


def reduce_quarters(keep, send):
    came = swap(send, "rep", 4, 1)
    low, high = add(keep[0], came[0]), add(keep[1], came[1])
    came = swap(high, "rep", 4, 2)
    count = BLOCKS
    for bit in (1, 2, 4):
        count //= 2
        low, high, came_low, came_high = low[:count], low[count:], came[:count], came[count:]
        low, high = add(low, came_low), add(high, came_high)
        came = swap(high, "shard", BLOCKS, bit)
    return add(low, came)[0]


def share_quarters(piece, rep):
    parts = [piece] + [swap(piece, "rep", 4, bit) for bit in (1, 2, 3)]
    out = []
    for place in range(4):
        pick = parts[3]
        for rel in range(3):
            pick = jnp.where(rep == place ^ rel, parts[rel], pick)
        out.append(pick.astype(F32))
    return out


def local(
    fast,
    tokens,
    lengths,
    w_qkv,
    b_query,
    b_value,
    w_out,
    b_out,
    ln1_gain,
    ln1_bias,
    w_up,
    b_up,
    w_down,
    b_down,
    ln2_gain,
    ln2_bias,
    cotangent,
):
    seqs, seq_len, width = tokens.shape
    rows = seqs * seq_len
    hidden_width = w_up.shape[1]
    half = width // 2
    groups = 3
    up_cut, out_cut = hidden_width // (2 * groups), half // groups
    vectors = (b_query, b_value, b_out, ln1_gain, ln1_bias, b_down, ln2_gain, ln2_bias, b_up)
    names = len(vectors)

    if fast:
        shard, rep = lax.axis_index("shard"), lax.axis_index("rep")
        x_at, core = rep // 2, rep % 2
    else:
        shard = rep = x_at = core = jnp.int32(0)
    block = width // BLOCKS
    quarter = block // 2
    meta = jnp.concatenate(
        [jnp.stack([shard, x_at, core]).astype(jnp.int32), lengths.astype(jnp.int32)]
    )

    def qkv_parts(w):
        return w.reshape(-1, 2, quarter, 3, 2, half)

    def up_parts(up, out):
        up = up.reshape(-1, 2, quarter, 2, groups, up_cut)
        out = out.reshape(-1, 2, quarter, 2, groups, out_cut)
        return jnp.concatenate([up, out], axis=-1)

    if fast:
        table = jnp.concatenate(vectors).reshape(1, -1)
        for bit in (4, 2, 1):
            table = jnp.concatenate([table, swap(table, "shard", BLOCKS, bit)], axis=0)
        table = jnp.take(table, turned(jnp.arange(BLOCKS) ^ shard), axis=0)

        def pick(array, axis_x, axis_core):
            array = lax.dynamic_index_in_dim(array, core, axis_core, keepdims=False)
            return lax.dynamic_index_in_dim(array, x_at, axis_x, keepdims=False)

        qkv_piece = pick(qkv_parts(w_qkv)[0], 0, 3).reshape(quarter, 3 * half)
        up_piece = pick(up_parts(w_up, w_out)[0], 0, 2).reshape(quarter, -1)
        down_piece = pick(w_down.reshape(2, 2, -1, width), 0, 0)
        qkv_w = gather_quarters(qkv_piece)
        up_w = gather_quarters(up_piece)
        down_w = gather_quarters(down_piece)
    else:
        everything = lambda a: lax.all_gather(a, "shard", axis=0, tiled=True)
        table = None
        full = [everything(v) for v in vectors]
        order = [turned(p) for p in range(BLOCKS)]
        both = lambda a: (a[0][:, order], a[1][:, order])
        qkv_w = both(
            qkv_parts(everything(w_qkv))
            .transpose(4, 1, 0, 2, 3, 5)
            .reshape(2, 2, BLOCKS, quarter, 3 * half)
        )
        up_w = both(
            up_parts(everything(w_up), everything(w_out))
            .transpose(3, 1, 0, 2, 4, 5)
            .reshape(2, 2, BLOCKS, quarter, -1)
        )
        down_w = both(
            everything(w_down).reshape(BLOCKS, 2, 2, -1, width).transpose(1, 2, 0, 3, 4)
        )
    if fast:
        full, start = [], 0
        for v in vectors:
            full.append(table[:, start : start + v.shape[0]].reshape(-1))
            start += v.shape[0]
    full = [v.astype(F32) for v in full]
    bias = jnp.stack(
        [full[0].reshape(2, half), jnp.zeros((2, half), F32), full[1].reshape(2, half)], axis=1
    ).reshape(2, 1, 3 * half)
    vec = jnp.stack(full[2:8] + [jnp.zeros_like(full[0])] * 2)

    qkv, mixed, lse = attend(meta, tokens, *qkv_w, bias)
    x_rows = tokens.reshape(rows, width)
    mixed_rows = mixed.reshape(rows, width)
    (
        layer_out,
        normed,
        active,
        grad_hidden,
        grad_second,
        grad_branch,
        grad_mixed,
        grad_vec,
        grad_b_up,
    ) = feed(
        meta,
        x_rows,
        mixed_rows,
        cotangent.reshape(rows, width),
        up_w,
        down_w,
        vec,
        full[8].reshape(1, -1),
        seq_len,
    )
    down_keep, down_send = grad_down(meta, active, grad_second)
    up_send = grad_up(1, meta, normed, mixed_rows, grad_hidden, grad_branch)
    up_keep = grad_up(0, meta, normed, mixed_rows, grad_hidden, grad_branch)
    grad_mixed = grad_mixed.reshape(seqs, seq_len, width)
    other_qkv, qkv_send, other_bias = attend_back(1, meta, tokens, qkv, mixed, grad_mixed, lse)
    mine_qkv, qkv_keep, mine_bias = attend_back(0, meta, tokens, qkv, mixed, grad_mixed, lse)
    input_grad = input_grad_of(
        meta,
        grad_branch,
        mine_qkv.reshape(rows, -1),
        other_qkv.reshape(rows, -1),
        *qkv_w,
    )

    bias_halves = jnp.stack([mine_bias, other_bias]).reshape(2, 3, half)
    bias_halves = jnp.where(core == 0, bias_halves, bias_halves[::-1])
    grad_vectors = [
        bias_halves[:, 0].reshape(-1),
        bias_halves[:, 2].reshape(-1),
        *[grad_vec[i] for i in range(6)],
        grad_b_up[0],
    ]
    if fast:
        total = jnp.concatenate([g.reshape(BLOCKS, -1) for g in grad_vectors], axis=1)
        for axis, size, bit in (
            ("rep", 4, 1),
            ("rep", 4, 2),
            ("shard", BLOCKS, 1),
            ("shard", BLOCKS, 2),
            ("shard", BLOCKS, 4),
        ):
            total = total + swap(total, axis, size, bit)
        total = lax.dynamic_index_in_dim(total, shard, 0, keepdims=False)
        sums, start = [], 0
        for v in vectors:
            sums.append(total[start : start + v.shape[0]])
            start += v.shape[0]
        down = share_quarters(reduce_quarters(down_keep, down_send), rep)
        up = share_quarters(reduce_quarters(up_keep, up_send), rep)
        qkv_sum = share_quarters(reduce_quarters(qkv_keep, qkv_send), rep)
        grad_w_down = jnp.stack(down).reshape(2, 2, -1, width).transpose(1, 0, 2, 3)
        grad_w_down = grad_w_down.reshape(-1, width)
        up = jnp.stack(up).reshape(2, 2, quarter, groups, up_cut + out_cut)
        up = up.transpose(0, 2, 1, 3, 4)
        grad_w_up = up[..., :up_cut].reshape(block, hidden_width)
        grad_w_out = up[..., up_cut:].reshape(block, width)
        qkv_sum = jnp.stack(qkv_sum).reshape(2, 2, quarter, 3, half)
        grad_w_qkv = qkv_sum.transpose(0, 2, 3, 1, 4).reshape(block, 3 * width)
    else:
        total_of = lambda a: lax.psum(
            lax.psum_scatter(a, "shard", scatter_dimension=0, tiled=True), "rep"
        )
        sums = [total_of(g) for g in grad_vectors]
        order = [turned(p) for p in range(BLOCKS)]
        down_keep, down_send, up_keep, up_send, qkv_keep, qkv_send = (
            a[:, order] for a in (down_keep, down_send, up_keep, up_send, qkv_keep, qkv_send)
        )
        down = jnp.stack([down_keep, down_send]).transpose(2, 0, 1, 3, 4)
        grad_w_down = total_of(down.reshape(hidden_width, width).astype(F32))
        up = jnp.stack([up_keep, up_send]).reshape(
            2, 2, BLOCKS, quarter, groups, up_cut + out_cut
        )
        up = up.transpose(2, 1, 3, 0, 4, 5)
        grad_w_up = total_of(up[..., :up_cut].reshape(width, hidden_width).astype(F32))
        grad_w_out = total_of(up[..., up_cut:].reshape(width, width).astype(F32))
        qkv_sum = jnp.stack([qkv_keep, qkv_send]).reshape(2, 2, BLOCKS, quarter, 3, half)
        qkv_sum = qkv_sum.transpose(2, 1, 3, 4, 0, 5).reshape(width, 3 * width)
        grad_w_qkv = total_of(qkv_sum.astype(F32))
    return (
        layer_out.reshape(seqs, seq_len, width),
        input_grad.reshape(seqs, seq_len, width),
        grad_w_qkv,
        sums[0],
        sums[1],
        grad_w_out,
        sums[2],
        sums[3],
        sums[4],
        grad_w_up,
        sums[8],
        grad_w_down,
        sums[5],
        sums[6],
        sums[7],
    )


def solution(mesh):
    fast = mesh.shape["shard"] == BLOCKS and mesh.shape["rep"] == 4
    by_seq = P(("shard", "rep"), None, None)
    one, two = P("shard"), P("shard", None)
    in_specs = (by_seq, P(("shard", "rep")), two, one, one, two, one, one, one)
    in_specs = in_specs + (two, one, two, one, one, one, by_seq)
    out_specs = (by_seq, by_seq, two, one, one, two, one, one, one, two, one, two, one, one, one)
    return jax.shard_map(
        functools.partial(local, fast),
        mesh=mesh,
        in_specs=in_specs,
        out_specs=out_specs,
        check_vma=False,
    )
```

time: 969 us -> 423 us (0.44)
  waiting for transfers between devices: 523 us -> 197 us
  matrix products: 192 us -> 0 us
  Pallas kernels: 0 us -> 140 us
  blocking collectives: 109 us -> 0 us
  local copies, waits for them, and re-layouts: 66.8 us -> 17.1 us
  starting transfers between devices: 0.36 us -> 42.5 us
  other arithmetic: 54.1 us -> 17.4 us
  between operations: 16.9 us -> 1.6 us
    reduce_scatter x3 -> x0, waiting for transfers between devices: 329 us -> none  [the longest x1 164 us: local(): lax.psum_scatter(grad_up, 'shard', scatter_dimension=0, tiled=True)]
    ppermute x0 -> x47, waiting for transfers between devices: none -> 197 us  [swap(): return lax.ppermute(array, axis, [(i, i ^ bit) for i in range(size)])]
    dot_general x26 -> x0, matrix products: 192 us -> none  [the longest x4 40.6 us: times_back(): lax.dot_general(left, right, (((1,), (1,)), ((), ())), preferred_element_...]
    pallas_call x0 -> x8, Pallas kernels: none -> 140 us  [the longest x1 48.8 us: feed(): pl.pallas_call(functools.partial(feed_kernel, seq_len), grid_spec=pltpu.P...]
    all_gather x4 -> x0, waiting for transfers between devices: 107 us -> none  [the longest x1 63 us: local(): lax.all_gather(w_up, 'shard', axis=0, tiled=True)]
    unnamed x2 -> x0, blocking collectives: 76.8 us -> none
    unnamed x10 -> x0, waiting for transfers between devices: 45.8 us -> none
    ppermute x0 -> x47, starting transfers between devices: none -> 42.5 us  [swap(): return lax.ppermute(array, axis, [(i, i ^ bit) for i in range(size)])]
  transfers between devices with their start and end apart: 9 -> 47, of which waited for: 6 -> 24; matrix products, arithmetic and copies ran while one was open for 25% -> 7% of each run, Pallas kernels for 0% -> 14%
where the time goes in v1:
time: 423 us; the launch traced here: 416 us
  waiting for transfers between devices  197 us (47%)
  Pallas kernels  140 us (33%)
  starting transfers between devices  42.5 us (10%)
  other arithmetic  17.4 us (4%)
  local copies, waits for them, and re-layouts  17.1 us (4%)
    ppermute x47, waiting for transfers between devices, swap(): return lax.ppermute(array, axis, [(i, i ^ bit) for i in range(size)])  197 us
    pallas_call x1, Pallas kernels, feed(): pl.pallas_call(functools.partial(feed_kernel, seq_len), grid_spec=pltpu.P...  48.8 us
    ppermute x47, starting transfers between devices, swap(): return lax.ppermute(array, axis, [(i, i ^ bit) for i in range(size)])  42.5 us
    pallas_call x2, Pallas kernels, attend_back(): pl.pallas_call(attend_back_kernel, grid_spec=pltpu.PrefetchScalarGridSpec...  32.6 us
    pallas_call x1, Pallas kernels, attend(): pl.pallas_call(attend_kernel, grid_spec=pltpu.PrefetchScalarGridSpec(num_...  19.9 us
    pallas_call x2, Pallas kernels, grad_up(): pl.pallas_call(grad_up_kernel, grid_spec=pltpu.PrefetchScalarGridSpec(num...  17.3 us
    pallas_call x1, Pallas kernels, grad_down(): pl.pallas_call(grad_down_kernel, grid_spec=pltpu.PrefetchScalarGridSpec(n...  11.8 us
    pallas_call x1, Pallas kernels, input_grad_of(): pl.pallas_call(input_kernel, grid_spec=pltpu.PrefetchScalarGridSpec(num_s...  10.1 us
  transfers between devices with their start and end apart: 47, of which 24 were waited for; matrix products, arithmetic and copies ran while one was open for 7% of the time, Pallas kernels for 14%

profile of v1, /device:TPU:0, one launch (start us, length us, event | category | flops | bytes accessed | tf_op | source)
XLA Modules:
  0.0 415.6 jit_solution(18440752891764015285)
XLA Ops:
  0.7 1.9 reshape.331
  3.1 4.1 collective-permute-start.8
  7.5 0.7 dynamic-slice_reduce_fusion
  8.3 3.0 collective-permute-start
  11.5 10.8 %collective-permute-done.8 = bf16[1,48,1920]{2,1,0:T(8,128)(2,1)S(1)} collective-permute-done((bf16[1,48,1920]{2,1,0:T(8,128)(2,1)S(1)}, bf16[1,48,1920]{2,1,0:T(8,128)(2,1)S(1)}, u32[]{:S(2)}, u32[]{:S(2)}) %collective-permute-start.8) | collective-permute-done | bytes 184352 | tf_op jit(solution)/shard_map/ppermute | solution.py:562
  22.5 12.5 %collective-permute-done.9 = bf16[2,48,1920]{2,1,0:T(8,128)(2,1)S(1)} collective-permute-done((bf16[2,48,1920]{2,1,0:T(8,128)(2,1)S(1)}, bf16[2,48,1920]{2,1,0:T(8,128)(2,1)S(1)}, u32[]{:S(2)}, u32[]{:S(2)}) %collective-permute-start.9) | collective-permute-done | bytes 368672 | tf_op jit(solution)/shard_map/ppermute | solution.py:562
  35.1 1.6 collective-permute-start.10
  36.9 2.1 collective-permute-start.14
  39.0 14.6 %collective-permute-done.10 = bf16[4,48,1920]{2,1,0:T(8,128)(2,1)S(1)} collective-permute-done((bf16[4,48,1920]{2,1,0:T(8,128)(2,1)S(1)}, bf16[4,48,1920]{2,1,0:T(8,128)(2,1)S(1)}, u32[]{:S(2)}, u32[]{:S(2)}) %collective-permute-start.10) | collective-permute-done | bytes 737312 | tf_op jit(solution)/shard_map/ppermute | solution.py:562
  53.6 1.6 collective-permute-start.11
  55.3 1.6 collective-permute-start.2
  57.6 10.9 %collective-permute-done.2 = bf16[4,48,1152]{2,1,0:T(8,128)(2,1)S(1)} collective-permute-done((bf16[4,48,1152]{2,1,0:T(8,128)(2,1)S(1)}, bf16[4,48,1152]{2,1,0:T(8,128)(2,1)S(1)}, u32[]{:S(2)}, u32[]{:S(2)}) %collective-permute-start.2) | collective-permute-done | bytes 442400 | tf_op jit(solution)/shard_map/ppermute | solution.py:562
  69.1 9.9 %collective-permute-done.15 = bf16[4,96,768]{2,1,0:T(8,128)(2,1)S(1)} collective-permute-done((bf16[4,96,768]{2,1,0:T(8,128)(2,1)S(1)}, bf16[4,96,768]{2,1,0:T(8,128)(2,1)S(1)}, u32[]{:S(2)}, u32[]{:S(2)}) %collective-permute-start.15) | collective-permute-done | bytes 589856 | tf_op jit(solution)/shard_map/ppermute | solution.py:562
  79.8 9.1 %collective-permute-done.11 = bf16[8,48,1920]{2,1,0:T(8,128)(2,1)S(1)} collective-permute-done((bf16[8,48,1920]{2,1,0:T(8,128)(2,1)S(1)}, bf16[8,48,1920]{2,1,0:T(8,128)(2,1)S(1)}, u32[]{:S(2)}, u32[]{:S(2)}) %collective-permute-start.11) | collective-permute-done | bytes 1474592 | tf_op jit(solution)/shard_map/ppermute | solution.py:562
  89.3 18.6 %collective-permute-done.3 = bf16[8,48,1152]{2,1,0:T(8,128)(2,1)S(1)} collective-permute-done((bf16[8,48,1152]{2,1,0:T(8,128)(2,1)S(1)}, bf16[8,48,1152]{2,1,0:T(8,128)(2,1)S(1)}, u32[]{:S(2)}, u32[]{:S(2)}) %collective-permute-start.3) | collective-permute-done | bytes 884768 | tf_op jit(solution)/shard_map/ppermute | solution.py:562
  107.9 1.4 pad_maximum_fusion.2.mine_ref.w_mine
  109.4 1.6 collective-permute-start.7
  111.0 20.3 %collective-permute-done.16 = bf16[8,96,768]{2,1,0:T(8,128)(2,1)S(1)} collective-permute-done((bf16[8,96,768]{2,1,0:T(8,128)(2,1)S(1)}, bf16[8,96,768]{2,1,0:T(8,128)(2,1)S(1)}, u32[]{:S(2)}, u32[]{:S(2)}) %collective-permute-start.16) | collective-permute-done | bytes 1179680 | tf_op jit(solution)/shard_map/ppermute | solution.py:562
  131.3 1.6 pad_maximum_fusion.1.down_mine
  137.0 19.9 %attend_forward.1 = (bf16[2,2,512,1152]{3,2,1,0:T(8,128)(2,1)}, bf16[2,512,768]{2,1,0:T(8,128)(2,1)}, f32[2,2,6,1,512]{4,3,2,1,0:T(1,128)}) custom-call(s32[5]{0:T(128)} %pad_add_fusion.meta, bf16[2,512,768]{2,1,0:T(8,128)(2,1)} %x_ref.1, bf16[2,8,48,1152]{3,2,1,0:T(8,128)(2,1)} %pad_maximum_fusion.2.mine_ref.w_mine, ...), custom_call_target="tpu_custom_call" | custom-call | flops 10066329600 | bytes 20000000 | tf_op jit(solution)/shard_map/attend_forward/pallas_call | solution.py:94
  156.8 48.8 %feed_forward_and_back.1 = (bf16[1024,768]{1,0:T(8,128)(2,1)}, bf16[1024,768]{1,0:T(8,128)(2,1)}, bf16[1024,3072]{1,0:T(8,128)(2,1)}, bf16[1024,3072]{1,0:T(8,12...) custom-call(s32[5]{0:T(128)} %pad_add_fusion.meta, ...), custom_call_target="tpu_custom_call" | custom-call | flops 21743271936 | bytes 40000000 | tf_op jit(solution)/shard_map/feed_forward_and_back/pallas_call | solution.py:286
  205.6 16.5 %attend_back.3 = (bf16[2,512,1152]{2,1,0:T(8,128)(2,1)}, bf16[2,8,48,1152]{3,2,1,0:T(8,128)(2,1)}, f32[1,1152]{1,0:T(1,128)}) custom-call(s32[5]{0:T(128)} %pad_add_fusion.meta, bf16[1024,768]{1,0:T(8,128)(2,1)} %bitcast.134, bf16[2,2,512,1152]{3,2,1,0:T(8,128)(2,1)} %get-tuple-element.38.qkv_ref, bf16[2,512,768]{2,1,0:T(8,128)(2,1)} %get-tuple-element.35.mixed_ref, ...), custom_call_target="tpu_custom_call" | custom-call | flops 9865003008 | bytes 16000000 | tf_op jit(solution)/shard_map/attend_back/pallas_call | solution.py:490
  222.1 16.1 %attend_back.2 = (bf16[2,512,1152]{2,1,0:T(8,128)(2,1)}, bf16[2,8,48,1152]{3,2,1,0:T(8,128)(2,1)}, f32[1,1152]{1,0:T(1,128)}) custom-call(s32[5]{0:T(128)} %pad_add_fusion.meta, bf16[1024,768]{1,0:T(8,128)(2,1)} %bitcast.135, bf16[2,2,512,1152]{3,2,1,0:T(8,128)(2,1)} %get-tuple-element.38.qkv_ref, bf16[2,512,768]{2,1,0:T(8,128)(2,1)} %get-tuple-element.35.mixed_ref, ...), custom_call_target="tpu_custom_call" | custom-call | flops 9865003008 | bytes 16000000 | tf_op jit(solution)/shard_map/attend_back/pallas_call | solution.py:490
  238.8 11.8 %grad_down.1 = (bf16[2,8,96,768]{3,2,1,0:T(8,128)(2,1)}, bf16[2,8,96,768]{3,2,1,0:T(8,128)(2,1)}) custom-call(s32[5]{0:T(128)} %pad_add_fusion.meta, bf16[1024,3072]{1,0:T(8,128)(2,1)} %get-tuple-element.51.active_ref, bf16[1024,768]{1,0:T(8,128)(2,1)} %get-tuple-element.52.grad_second_ref), custom_call_target="tpu_custom_call" | custom-call | flops 4831838208 | bytes 16000000 | tf_op jit(solution)/shard_map/grad_down/pallas_call | solution.py:402
  250.6 8.7 %grad_up.3 = bf16[2,8,48,1920]{3,2,1,0:T(8,128)(2,1)} custom-call(s32[5]{0:T(128)} %pad_add_fusion.meta, bf16[1024,768]{1,0:T(8,128)(2,1)} %get-tuple-element.49.norm_ref, bf16[1024,768]{1,0:T(8,128)(2,1)} %bitcast.121, bf16[1024,3072]{1,0:T(8,128)(2,1)} %get-tuple-element.50.grad_hidden_ref, bf16[1024,768]{1,0:T(8,128)(2,1)} %get-tuple-element.37.branch_ref.grad_branch_ref), custom_call_target="tpu_custom_call" | custom-call | flops 3019898880 | bytes 12000000 | tf_op jit(solution)/shard_map/grad_up/pallas_call | solution.py:360
  261.9 2.9 collective-permute-done.26
  264.9 1.6 collective-permute-start.27
  266.4 2.4 collective-permute-done.27
  268.8 1.6 collective-permute-start.28
  270.4 2.4 collective-permute-done.28
  272.8 10.1 %input_grad.1 = f32[1024,768]{1,0:T(8,128)} custom-call(s32[5]{0:T(128)} %pad_add_fusion.meta, bf16[1024,768]{1,0:T(8,128)(2,1)} %get-tuple-element.37.branch_ref.grad_branch_ref, bf16[1024,1152]{1,0:T(8,128)(2,1)} %bitcast.138, bf16[1024,1152]{1,0:T(8,128)(2,1)} %bitcast.137, bf16[2,8,48,1152]{3,2,1,0:T(8,128)(2,1)} %pad_maximum_fusion.2.mine_ref.w_mine, ...), custom_call_target="tpu_custom_call" | custom-call | flops 3623878656 | bytes 14000000 | tf_op jit(solution)/shard_map/input_grad/pallas_call | solution.py:545
  283.0 4.1 collective-permute-start.30
  287.1 2.8 add_convert_fusion.5
  289.9 1.5 collective-permute-start.19
  291.4 8.6 %grad_up.2 = bf16[2,8,48,1920]{3,2,1,0:T(8,128)(2,1)} custom-call(s32[5]{0:T(128)} %pad_add_fusion.meta, bf16[1024,768]{1,0:T(8,128)(2,1)} %get-tuple-element.49.norm_ref, bf16[1024,768]{1,0:T(8,128)(2,1)} %bitcast.122, bf16[1024,3072]{1,0:T(8,128)(2,1)} %get-tuple-element.50.grad_hidden_ref, bf16[1024,768]{1,0:T(8,128)(2,1)} %get-tuple-element.37.branch_ref.grad_branch_ref), custom_call_target="tpu_custom_call" | custom-call | flops 3019898880 | bytes 12000000 | tf_op jit(solution)/shard_map/grad_up/pallas_call | solution.py:360
  300.6 3.2 add_convert_fusion.3
  304.4 8.4 %collective-permute-done.19 = bf16[8,48,1152]{2,1,0:T(8,128)(2,1)} collective-permute-done((bf16[8,48,1152]{2,1,0:T(8,128)(2,1)}, bf16[8,48,1152]{2,1,0:T(8,128)(2,1)}, u32[]{:S(2)}, u32[]{:S(2)}) %collective-permute-start.19) | collective-permute-done | bytes 884768 | tf_op jit(solution)/shard_map/ppermute | solution.py:562
  312.8 1.4 fusion.8
  314.1 1.6 collective-permute-start.20
  315.7 0.8 add_convert_fusion.1
  316.5 1.6 collective-permute-start.32
  318.0 4.4 %collective-permute-done.20 = bf16[4,48,1152]{2,1,0:T(8,128)(2,1)S(1)} collective-permute-done((bf16[4,48,1152]{2,1,0:T(8,128)(2,1)S(1)}, bf16[4,48,1152]{2,1,0:T(8,128)(2,1)S(1)}, u32[]{:S(2)}, u32[]{:S(2)}) %collective-permute-start.20) | collective-permute-done | bytes 442400 | tf_op jit(solution)/shard_map/ppermute | solution.py:562
  323.3 5.3 %collective-permute-done.21 = bf16[2,48,1152]{2,1,0:T(8,128)(2,1)S(1)} collective-permute-done((bf16[2,48,1152]{2,1,0:T(8,128)(2,1)S(1)}, bf16[2,48,1152]{2,1,0:T(8,128)(2,1)S(1)}, u32[]{:S(2)}, u32[]{:S(2)}) %collective-permute-start.21) | collective-permute-done | bytes 221216 | tf_op jit(solution)/shard_map/ppermute | solution.py:562
  328.7 9.2 %collective-permute-done.40 = bf16[8,96,768]{2,1,0:T(8,128)(2,1)S(1)} collective-permute-done((bf16[8,96,768]{2,1,0:T(8,128)(2,1)S(1)}, bf16[8,96,768]{2,1,0:T(8,128)(2,1)S(1)}, u32[]{:S(2)}, u32[]{:S(2)}) %collective-permute-start.40) | collective-permute-done | bytes 1179680 | tf_op jit(solution)/shard_map/ppermute | solution.py:562
  338.2 1.6 collective-permute-start.41
  339.9 1.6 collective-permute-start.23
  342.1 26.2 %collective-permute-done.32 = bf16[8,48,1920]{2,1,0:T(8,128)(2,1)S(1)} collective-permute-done((bf16[8,48,1920]{2,1,0:T(8,128)(2,1)S(1)}, bf16[8,48,1920]{2,1,0:T(8,128)(2,1)S(1)}, u32[]{:S(2)}, u32[]{:S(2)}) %collective-permute-start.32) | collective-permute-done | bytes 1474592 | tf_op jit(solution)/shard_map/ppermute | solution.py:562
  368.8 1.6 collective-permute-start.33
  371.0 8.8 %collective-permute-done.42 = bf16[2,96,768]{2,1,0:T(8,128)(2,1)S(1)} collective-permute-done((bf16[2,96,768]{2,1,0:T(8,128)(2,1)S(1)}, bf16[2,96,768]{2,1,0:T(8,128)(2,1)S(1)}, u32[]{:S(2)}, u32[]{:S(2)}) %collective-permute-start.42) | collective-permute-done | bytes 294944 | tf_op jit(solution)/shard_map/ppermute | solution.py:562
  379.8 0.7 add_convert_fusion.16
  380.6 0.8 collective-permute-done.33
  383.4 1.6 reshape.360
  385.0 3.1 collective-permute-done.43
  388.1 1.0 fusion.11
  389.1 1.5 collective-permute-start.44
  391.5 3.6 collective-permute-done.44
  395.0 1.8 collective-permute-done.46
  396.9 4.3 %collective-permute-done.35 = bf16[1,48,1920]{2,1,0:T(8,128)(2,1)S(1)} collective-permute-done((bf16[1,48,1920]{2,1,0:T(8,128)(2,1)S(1)}, bf16[1,48,1920]{2,1,0:T(8,128)(2,1)S(1)}, u32[]{:S(2)}, u32[]{:S(2)}) %collective-permute-start.35) | collective-permute-done | bytes 184352 | tf_op jit(solution)/shard_map/ppermute | solution.py:562
  401.3 1.5 collective-permute-start.36
  403.6 1.1 copy.54
  404.7 4.1 collective-permute-done.36
  408.9 2.1 collective-permute-done.38
  412.7 1.7 reshape.344
  414.5 0.9 reshape.343
  (202 shorter events, 21.0 us)
Async XLA Ops:
  2.7 8.5 %copy-start.15 = (bf16[384]{0:T(512)(128)(2,1)S(1)}, bf16[384]{0:T(512)(128)(2,1)}, u32[]{:S(2)}) copy-start(bf16[384]{0:T(512)(128)(2,1)} %param.26) | copy-start | bytes 2308
  2.7 8.5 %copy-start.16 = (bf16[96]{0:T(256)(128)(2,1)S(1)}, bf16[96]{0:T(256)(128)(2,1)}, u32[]{:S(2)}) copy-start(bf16[96]{0:T(256)(128)(2,1)} %param.19) | copy-start | bytes 580
  2.7 8.5 %copy-start.17 = (bf16[96]{0:T(256)(128)(2,1)S(1)}, bf16[96]{0:T(256)(128)(2,1)}, u32[]{:S(2)}) copy-start(bf16[96]{0:T(256)(128)(2,1)} %param.20) | copy-start | bytes 580
  2.8 8.5 %copy-start.18 = (bf16[96]{0:T(256)(128)(2,1)S(1)}, bf16[96]{0:T(256)(128)(2,1)}, u32[]{:S(2)}) copy-start(bf16[96]{0:T(256)(128)(2,1)} %param.22) | copy-start | bytes 580
  2.8 8.5 %copy-start.19 = (bf16[96]{0:T(256)(128)(2,1)S(1)}, bf16[96]{0:T(256)(128)(2,1)}, u32[]{:S(2)}) copy-start(bf16[96]{0:T(256)(128)(2,1)} %param.23) | copy-start | bytes 580
  2.8 8.5 %copy-start.20 = (bf16[96]{0:T(256)(128)(2,1)S(1)}, bf16[96]{0:T(256)(128)(2,1)}, u32[]{:S(2)}) copy-start(bf16[96]{0:T(256)(128)(2,1)} %param.24) | copy-start | bytes 580
  2.8 8.5 %copy-start.21 = (bf16[96]{0:T(256)(128)(2,1)S(1)}, bf16[96]{0:T(256)(128)(2,1)}, u32[]{:S(2)}) copy-start(bf16[96]{0:T(256)(128)(2,1)} %param.28) | copy-start | bytes 580
  2.8 8.5 %copy-start.22 = (bf16[96]{0:T(256)(128)(2,1)S(1)}, bf16[96]{0:T(256)(128)(2,1)}, u32[]{:S(2)}) copy-start(bf16[96]{0:T(256)(128)(2,1)} %param.29) | copy-start | bytes 580
  3.1 19.1 %collective-permute-start.8 = (bf16[1,48,1920]{2,1,0:T(8,128)(2,1)S(1)}, bf16[1,48,1920]{2,1,0:T(8,128)(2,1)S(1)}, u32[]{:S(2)}, u32[]{:S(2)}) collective-permute-start(bf16[1,48,1920]{2,1,0:T(8,128)(2,1)S(1)} %broadcast_in_dim_reshape.7), channel_id=1, source_target_pairs={{0,16},{4,20},{8,24},{12,28},{16,0},{20,4},{24,8},{28,12},{1,17},{... | collective-permute-start | bytes 552968 | tf_op jit(solution)/shard_map/ppermute | solution.py:562
  7.2 29.6 %collective-permute-start.13 = (bf16[1,96,768]{2,1,0:T(8,128)(2,1)S(1)}, bf16[1,96,768]{2,1,0:T(8,128)(2,1)S(1)}, u32[]{:S(2)}, u32[]{:S(2)}) collective-permute-start(bf16[1,96,768]{2,1,0:T(8,128)(2,1)S(1)} %dynamic-slice_bitcast_fusion), channel_id=1, source_target_pairs={{0,16},{4,20},{8,24},{12,28},{16,0},{20,4},{24,8},{28,12},{1,17},{... | collective-permute-start | bytes 442376 | tf_op jit(solution)/shard_map/ppermute | solution.py:562
  8.3 28.4 %collective-permute-start = (bf16[1,48,1152]{2,1,0:T(8,128)(2,1)S(1)}, bf16[1,48,1152]{2,1,0:T(8,128)(2,1)S(1)}, u32[]{:S(2)}, u32[]{:S(2)}) collective-permute-start(bf16[1,48,1152]{2,1,0:T(8,128)(2,1)S(1)} %broadcast_in_dim_reshape.6), channel_id=1, source_target_pairs={{0,16},{4,20},{8,24},{12,28},{16,0},{20,4},{24,8},{28,12},{1,17},{... | collective-permute-start | bytes 331784 | tf_op jit(solution)/shard_map/ppermute | solution.py:562
  11.4 68.3 %collective-permute-start.5 = (bf16[1,1152]{1,0:T(2,128)(2,1)S(1)}, bf16[1,1152]{1,0:T(2,128)(2,1)S(1)}, u32[]{:S(2)}, u32[]{:S(2)}) collective-permute-start(bf16[1,1152]{1,0:T(2,128)(2,1)S(1)} %reshape.327), channel_id=1, source_target_pairs={{0,16},{4,20},{8,24},{12,28},{16,0},{20,4},{24,8},{28,12},{1,17},{... | collective-permute-start | bytes 6920 | tf_op jit(solution)/shard_map/ppermute | solution.py:562
  22.3 12.7 %collective-permute-start.9 = (bf16[2,48,1920]{2,1,0:T(8,128)(2,1)S(1)}, bf16[2,48,1920]{2,1,0:T(8,128)(2,1)S(1)}, u32[]{:S(2)}, u32[]{:S(2)}) collective-permute-start(bf16[2,48,1920]{2,1,0:T(8,128)(2,1)S(1)} %pad_maximum_fusion.8), channel_id=1, source_target_pairs={{0,8},{4,12},{8,0},{12,4},{16,24},{20,28},{24,16},{28,20},{1,9},{5... | collective-permute-start | bytes 1105928 | tf_op jit(solution)/shard_map/ppermute | solution.py:562
  35.1 18.5 %collective-permute-start.10 = (bf16[4,48,1920]{2,1,0:T(8,128)(2,1)S(1)}, bf16[4,48,1920]{2,1,0:T(8,128)(2,1)S(1)}, u32[]{:S(2)}, u32[]{:S(2)}) collective-permute-start(bf16[4,48,1920]{2,1,0:T(8,128)(2,1)S(1)} %pad_maximum_fusion.4), channel_id=1, source_target_pairs={{0,4},{4,0},{8,12},{12,8},{16,20},{20,16},{24,28},{28,24},{1,5},{5... | collective-permute-start | bytes 2211848 | tf_op jit(solution)/shard_map/ppermute | solution.py:562
  36.7 18.5 %collective-permute-start.1 = (bf16[2,48,1152]{2,1,0:T(8,128)(2,1)S(1)}, bf16[2,48,1152]{2,1,0:T(8,128)(2,1)S(1)}, u32[]{:S(2)}, u32[]{:S(2)}) collective-permute-start(bf16[2,48,1152]{2,1,0:T(8,128)(2,1)S(1)} %pad_maximum_fusion.10), channel_id=1, source_target_pairs={{0,8},{4,12},{8,0},{12,4},{16,24},{20,28},{24,16},{28,20},{1,9},{5... | collective-permute-start | bytes 663560 | tf_op jit(solution)/shard_map/ppermute | solution.py:562
  36.9 20.0 %collective-permute-start.14 = (bf16[2,96,768]{2,1,0:T(8,128)(2,1)S(1)}, bf16[2,96,768]{2,1,0:T(8,128)(2,1)S(1)}, u32[]{:S(2)}, u32[]{:S(2)}) collective-permute-start(bf16[2,96,768]{2,1,0:T(8,128)(2,1)S(1)} %pad_maximum_fusion.9), channel_id=1, source_target_pairs={{0,8},{4,12},{8,0},{12,4},{16,24},{20,28},{24,16},{28,20},{1,9},{5... | collective-permute-start | bytes 884744 | tf_op jit(solution)/shard_map/ppermute | solution.py:562
  53.6 14.9 %copy-start.4 = (bf16[8,48,1920]{2,1,0:T(8,128)(2,1)}, bf16[8,48,1920]{2,1,0:T(8,128)(2,1)S(1)}, u32[]{:S(2)}) copy-start(bf16[8,48,1920]{2,1,0:T(8,128)(2,1)S(1)} %constant_dynamic-update-slice_fusion.4) | copy-start | bytes 4423684
  53.6 35.3 %collective-permute-start.11 = (bf16[8,48,1920]{2,1,0:T(8,128)(2,1)S(1)}, bf16[8,48,1920]{2,1,0:T(8,128)(2,1)S(1)}, u32[]{:S(2)}, u32[]{:S(2)}) collective-permute-start(bf16[8,48,1920]{2,1,0:T(8,128)(2,1)S(1)} %constant_dynamic-update-slice_fusion.4), channel_id=1, source_target_pairs={{0,2},{1,3},{2,0},{3,1},{4,6},{5,7},{6,4},{7,5},{8,10},{9,11},{10,... | collective-permute-start | bytes 4423688 | tf_op jit(solution)/shard_map/ppermute | solution.py:562
  55.3 13.2 %collective-permute-start.2 = (bf16[4,48,1152]{2,1,0:T(8,128)(2,1)S(1)}, bf16[4,48,1152]{2,1,0:T(8,128)(2,1)S(1)}, u32[]{:S(2)}, u32[]{:S(2)}) collective-permute-start(bf16[4,48,1152]{2,1,0:T(8,128)(2,1)S(1)} %pad_maximum_fusion.7), channel_id=1, source_target_pairs={{0,4},{4,0},{8,12},{12,8},{16,20},{20,16},{24,28},{28,24},{1,5},{5... | collective-permute-start | bytes 1327112 | tf_op jit(solution)/shard_map/ppermute | solution.py:562
  57.0 22.0 %collective-permute-start.15 = (bf16[4,96,768]{2,1,0:T(8,128)(2,1)S(1)}, bf16[4,96,768]{2,1,0:T(8,128)(2,1)S(1)}, u32[]{:S(2)}, u32[]{:S(2)}) collective-permute-start(bf16[4,96,768]{2,1,0:T(8,128)(2,1)S(1)} %pad_maximum_fusion.5), channel_id=1, source_target_pairs={{0,4},{4,0},{8,12},{12,8},{16,20},{20,16},{24,28},{28,24},{1,5},{5... | collective-permute-start | bytes 1769480 | tf_op jit(solution)/shard_map/ppermute | solution.py:562
  68.5 39.4 %collective-permute-start.3 = (bf16[8,48,1152]{2,1,0:T(8,128)(2,1)S(1)}, bf16[8,48,1152]{2,1,0:T(8,128)(2,1)S(1)}, u32[]{:S(2)}, u32[]{:S(2)}) collective-permute-start(bf16[8,48,1152]{2,1,0:T(8,128)(2,1)S(1)} %constant_dynamic-update-slice_fusion), channel_id=1, source_target_pairs={{0,2},{1,3},{2,0},{3,1},{4,6},{5,7},{6,4},{7,5},{8,10},{9,11},{10,... | collective-permute-start | bytes 2654216 | tf_op jit(solution)/shard_map/ppermute | solution.py:562
  69.1 19.8 %copy-start.5 = (bf16[8,48,1920]{2,1,0:T(8,128)(2,1)S(1)}, bf16[8,48,1920]{2,1,0:T(8,128)(2,1)}, u32[]{:S(2)}) copy-start(bf16[8,48,1920]{2,1,0:T(8,128)(2,1)} %copy-done.4) | copy-start | bytes 4423684
  79.2 52.1 %collective-permute-start.16 = (bf16[8,96,768]{2,1,0:T(8,128)(2,1)S(1)}, bf16[8,96,768]{2,1,0:T(8,128)(2,1)S(1)}, u32[]{:S(2)}, u32[]{:S(2)}) collective-permute-start(bf16[8,96,768]{2,1,0:T(8,128)(2,1)S(1)} %get-tuple-element.80), channel_id=1, source_target_pairs={{0,2},{1,3},{2,0},{3,1},{4,6},{5,7},{6,4},{7,5},{8,10},{9,11},{10,... | collective-permute-start | bytes 3538952 | tf_op jit(solution)/shard_map/ppermute | solution.py:562
  79.8 29.6 %collective-permute-start.6 = (bf16[2,1152]{1,0:T(2,128)(2,1)S(1)}, bf16[2,1152]{1,0:T(2,128)(2,1)S(1)}, u32[]{:S(2)}, u32[]{:S(2)}) collective-permute-start(bf16[2,1152]{1,0:T(2,128)(2,1)S(1)} %pad_maximum_fusion.14), channel_id=1, source_target_pairs={{0,8},{4,12},{8,0},{12,4},{16,24},{20,28},{24,16},{28,20},{1,9},{5... | collective-permute-start | bytes 13832 | tf_op jit(solution)/shard_map/ppermute | solution.py:562
  89.2 20.1 %copy-start.3 = (bf16[2,8,48,1920]{3,2,1,0:T(8,128)(2,1)}, bf16[2,8,48,1920]{3,2,1,0:T(8,128)(2,1)S(1)}, u32[]{:S(2)}) copy-start(bf16[2,8,48,1920]{3,2,1,0:T(8,128)(2,1)S(1)} %pad_maximum_fusion.up_mine) | copy-start | bytes 8847364
  89.2 67.6 %collective-permute-start.12 = (bf16[2,8,48,1920]{3,2,1,0:T(8,128)(2,1)S(1)}, bf16[2,8,48,1920]{3,2,1,0:T(8,128)(2,1)}, u32[]{:S(2)}, u32[]{:S(2)}) collective-permute-start(bf16[2,8,48,1920]{3,2,1,0:T(8,128)(2,1)S(1)} %pad_maximum_fusion.up_mine), channel_id=1, source_target_pairs={{0,1},{1,0},{2,3},{3,2},{4,5},{5,4},{6,7},{7,6},{8,9},{9,8},{10,11... | collective-permute-start | bytes 8847368 | tf_op jit(solution)/shard_map/ppermute | solution.py:562
  109.3 27.6 %collective-permute-start.4 = (bf16[2,8,48,1152]{3,2,1,0:T(8,128)(2,1)}, bf16[2,8,48,1152]{3,2,1,0:T(8,128)(2,1)}, u32[]{:S(2)}, u32[]{:S(2)}) collective-permute-start(bf16[2,8,48,1152]{3,2,1,0:T(8,128)(2,1)} %pad_maximum_fusion.2.mine_ref.w_mine), channel_id=1, source_target_pairs={{0,1},{1,0},{2,3},{3,2},{4,5},{5,4},{6,7},{7,6},{8,9},{9,8},{10,11... | collective-permute-start | bytes 5308424 | tf_op jit(solution)/shard_map/ppermute | solution.py:562
  109.4 24.2 %collective-permute-start.7 = (bf16[4,1152]{1,0:T(4,128)(2,1)S(1)}, bf16[4,1152]{1,0:T(4,128)(2,1)S(1)}, u32[]{:S(2)}, u32[]{:S(2)}) collective-permute-start(bf16[4,1152]{1,0:T(4,128)(2,1)S(1)} %pad_maximum_fusion.13), channel_id=1, source_target_pairs={{0,4},{4,0},{8,12},{12,8},{16,20},{20,16},{24,28},{28,24},{1,5},{5... | collective-permute-start | bytes 27656 | tf_op jit(solution)/shard_map/ppermute | solution.py:562
  132.9 23.9 %collective-permute-start.17 = (bf16[2,8,96,768]{3,2,1,0:T(8,128)(2,1)}, bf16[2,8,96,768]{3,2,1,0:T(8,128)(2,1)}, u32[]{:S(2)}, u32[]{:S(2)}) collective-permute-start(bf16[2,8,96,768]{3,2,1,0:T(8,128)(2,1)} %pad_maximum_fusion.1.down_mine), channel_id=1, source_target_pairs={{0,1},{1,0},{2,3},{3,2},{4,5},{5,4},{6,7},{7,6},{8,9},{9,8},{10,11... | collective-permute-start | bytes 7077896 | tf_op jit(solution)/shard_map/ppermute | solution.py:562
  238.2 48.9 %collective-permute-start.18 = (bf16[2,8,48,1152]{3,2,1,0:T(8,128)(2,1)}, bf16[2,8,48,1152]{3,2,1,0:T(8,128)(2,1)}, u32[]{:S(2)}, u32[]{:S(2)}) collective-permute-start(bf16[2,8,48,1152]{3,2,1,0:T(8,128)(2,1)} %get-tuple-element.44), channel_id=1, source_target_pairs={{0,1},{1,0},{2,3},{3,2},{4,5},{5,4},{6,7},{7,6},{8,9},{9,8},{10,11... | collective-permute-start | bytes 5308424 | tf_op jit(solution)/shard_map/ppermute | solution.py:562
  250.6 50.0 %collective-permute-start.39 = (bf16[2,8,96,768]{3,2,1,0:T(8,128)(2,1)}, bf16[2,8,96,768]{3,2,1,0:T(8,128)(2,1)}, u32[]{:S(2)}, u32[]{:S(2)}) collective-permute-start(bf16[2,8,96,768]{3,2,1,0:T(8,128)(2,1)} %get-tuple-element.54), channel_id=1, source_target_pairs={{0,1},{1,0},{2,3},{3,2},{4,5},{5,4},{6,7},{7,6},{8,9},{9,8},{10,11... | collective-permute-start | bytes 7077896 | tf_op jit(solution)/shard_map/ppermute | solution.py:562
  250.6 9.2 %copy-start.13 = (f32[1,1152]{1,0:T(1,128)S(1)}, f32[1,1152]{1,0:T(1,128)}, u32[]{:S(2)}) copy-start(f32[1,1152]{1,0:T(1,128)} %get-tuple-element.46) | copy-start | bytes 13828
  250.6 9.2 %copy-start.14 = (f32[1,1152]{1,0:T(1,128)S(1)}, f32[1,1152]{1,0:T(1,128)}, u32[]{:S(2)}) copy-start(f32[1,1152]{1,0:T(1,128)} %get-tuple-element.45) | copy-start | bytes 13828
  250.6 9.5 %copy-start.11 = (f32[8,768]{1,0:T(8,128)S(1)}, f32[8,768]{1,0:T(8,128)}, u32[]{:S(2)}) copy-start(f32[8,768]{1,0:T(8,128)} %get-tuple-element.47) | copy-start | bytes 73732
  250.6 10.5 %copy-start.12 = (f32[1,3072]{1,0:T(1,128)S(1)}, f32[1,3072]{1,0:T(1,128)}, u32[]{:S(2)}) copy-start(f32[1,3072]{1,0:T(1,128)} %get-tuple-element.48) | copy-start | bytes 36868
  259.3 56.4 %collective-permute-start.31 = (bf16[2,8,48,1920]{3,2,1,0:T(8,128)(2,1)}, bf16[2,8,48,1920]{3,2,1,0:T(8,128)(2,1)S(1)}, u32[]{:S(2)}, u32[]{:S(2)}) collective-permute-start(bf16[2,8,48,1920]{3,2,1,0:T(8,128)(2,1)} %grad_up.3), channel_id=1, source_target_pairs={{0,1},{1,0},{2,3},{3,2},{4,5},{5,4},{6,7},{7,6},{8,9},{9,8},{10,11... | collective-permute-start | bytes 8847368 | tf_op jit(solution)/shard_map/ppermute | solution.py:562
  261.9 2.9 collective-permute-start.26
  264.9 4.0 collective-permute-start.27
  268.8 4.0 collective-permute-start.28
  272.8 10.1 %collective-permute-start.29 = (f32[8,1152]{1,0:T(8,128)S(1)}, f32[8,1152]{1,0:T(8,128)S(1)}, u32[]{:S(2)}, u32[]{:S(2)}) collective-permute-start(f32[8,1152]{1,0:T(8,128)S(1)} %add.173), channel_id=1, source_target_pairs={{0,8},{4,12},{8,0},{12,4},{16,24},{20,28},{24,16},{28,20},{1,9},{5... | collective-permute-start | bytes 110600 | tf_op jit(solution)/shard_map/ppermute | solution.py:562
  272.8 14.3 %copy-start.6 = (bf16[2,8,48,1152]{3,2,1,0:T(8,128)(2,1)S(1)}, bf16[2,8,48,1152]{3,2,1,0:T(8,128)(2,1)}, u32[]{:S(2)}) copy-start(bf16[2,8,48,1152]{3,2,1,0:T(8,128)(2,1)} %get-tuple-element.43) | copy-start | bytes 5308420
  283.0 17.0 %collective-permute-start.30 = (f32[8,1152]{1,0:T(8,128)S(1)}, f32[8,1152]{1,0:T(8,128)S(1)}, u32[]{:S(2)}, u32[]{:S(2)}) collective-permute-start(f32[8,1152]{1,0:T(8,128)S(1)} %add.174), channel_id=1, source_target_pairs={{0,16},{4,20},{8,24},{12,28},{16,0},{20,4},{24,8},{28,12},{1,17},{... | collective-permute-start | bytes 110600 | tf_op jit(solution)/shard_map/ppermute | solution.py:562
  289.9 22.9 %collective-permute-start.19 = (bf16[8,48,1152]{2,1,0:T(8,128)(2,1)}, bf16[8,48,1152]{2,1,0:T(8,128)(2,1)}, u32[]{:S(2)}, u32[]{:S(2)}) collective-permute-start(bf16[8,48,1152]{2,1,0:T(8,128)(2,1)} %get-tuple-element.68), channel_id=1, source_target_pairs={{0,2},{1,3},{2,0},{3,1},{4,6},{5,7},{6,4},{7,5},{8,10},{9,11},{10,... | collective-permute-start | bytes 2654216 | tf_op jit(solution)/shard_map/ppermute | solution.py:562
  300.6 15.2 %copy-start.2 = (bf16[2,8,48,1920]{3,2,1,0:T(8,128)(2,1)S(1)}, bf16[2,8,48,1920]{3,2,1,0:T(8,128)(2,1)}, u32[]{:S(2)}) copy-start(bf16[2,8,48,1920]{3,2,1,0:T(8,128)(2,1)} %grad_up.2) | copy-start | bytes 8847364
  303.8 34.2 %collective-permute-start.40 = (bf16[8,96,768]{2,1,0:T(8,128)(2,1)S(1)}, bf16[8,96,768]{2,1,0:T(8,128)(2,1)S(1)}, u32[]{:S(2)}, u32[]{:S(2)}) collective-permute-start(bf16[8,96,768]{2,1,0:T(8,128)(2,1)S(1)} %get-tuple-element.66), channel_id=1, source_target_pairs={{0,2},{1,3},{2,0},{3,1},{4,6},{5,7},{6,4},{7,5},{8,10},{9,11},{10,... | collective-permute-start | bytes 3538952 | tf_op jit(solution)/shard_map/ppermute | solution.py:562
  314.1 8.4 %collective-permute-start.20 = (bf16[4,48,1152]{2,1,0:T(8,128)(2,1)S(1)}, bf16[4,48,1152]{2,1,0:T(8,128)(2,1)S(1)}, u32[]{:S(2)}, u32[]{:S(2)}) collective-permute-start(bf16[4,48,1152]{2,1,0:T(8,128)(2,1)S(1)} %get-tuple-element.74), channel_id=1, source_target_pairs={{0,4},{4,0},{8,12},{12,8},{16,20},{20,16},{24,28},{28,24},{1,5},{5... | collective-permute-start | bytes 1327112 | tf_op jit(solution)/shard_map/ppermute | solution.py:562
  316.5 51.9 %collective-permute-start.32 = (bf16[8,48,1920]{2,1,0:T(8,128)(2,1)S(1)}, bf16[8,48,1920]{2,1,0:T(8,128)(2,1)S(1)}, u32[]{:S(2)}, u32[]{:S(2)}) collective-permute-start(bf16[8,48,1920]{2,1,0:T(8,128)(2,1)S(1)} %get-tuple-element.64), channel_id=1, source_target_pairs={{0,2},{1,3},{2,0},{3,1},{4,6},{5,7},{6,4},{7,5},{8,10},{9,11},{10,... | collective-permute-start | bytes 4423688 | tf_op jit(solution)/shard_map/ppermute | solution.py:562
  322.6 6.0 %collective-permute-start.21 = (bf16[2,48,1152]{2,1,0:T(8,128)(2,1)S(1)}, bf16[2,48,1152]{2,1,0:T(8,128)(2,1)S(1)}, u32[]{:S(2)}, u32[]{:S(2)}) collective-permute-start(bf16[2,48,1152]{2,1,0:T(8,128)(2,1)S(1)} %get-tuple-element.82), channel_id=1, source_target_pairs={{0,8},{4,12},{8,0},{12,4},{16,24},{20,28},{24,16},{28,20},{1,9},{5... | collective-permute-start | bytes 663560 | tf_op jit(solution)/shard_map/ppermute | solution.py:562
  328.6 11.2 %collective-permute-start.22 = (bf16[1,48,1152]{2,1,0:T(8,128)(2,1)S(1)}, bf16[1,48,1152]{2,1,0:T(8,128)(2,1)S(1)}, u32[]{:S(2)}, u32[]{:S(2)}) collective-permute-start(bf16[1,48,1152]{2,1,0:T(8,128)(2,1)S(1)} %add_convert_fusion.19), channel_id=1, source_target_pairs={{0,16},{4,20},{8,24},{12,28},{16,0},{20,4},{24,8},{28,12},{1,17},{... | collective-permute-start | bytes 331784 | tf_op jit(solution)/shard_map/ppermute | solution.py:562
  338.2 32.1 %collective-permute-start.41 = (bf16[4,96,768]{2,1,0:T(8,128)(2,1)S(1)}, bf16[4,96,768]{2,1,0:T(8,128)(2,1)S(1)}, u32[]{:S(2)}, u32[]{:S(2)}) collective-permute-start(bf16[4,96,768]{2,1,0:T(8,128)(2,1)S(1)} %get-tuple-element.72), channel_id=1, source_target_pairs={{0,4},{4,0},{8,12},{12,8},{16,20},{20,16},{24,28},{28,24},{1,5},{5... | collective-permute-start | bytes 1769480 | tf_op jit(solution)/shard_map/ppermute | solution.py:562
  339.9 31.0 %collective-permute-start.23 = (bf16[48,1152]{1,0:T(8,128)(2,1)S(1)}, bf16[48,1152]{1,0:T(8,128)(2,1)S(1)}, u32[]{:S(2)}, u32[]{:S(2)}) collective-permute-start(bf16[48,1152]{1,0:T(8,128)(2,1)S(1)} %fusion.12), channel_id=1, source_target_pairs={{0,2},{1,3},{2,0},{3,1},{4,6},{5,7},{6,4},{7,5},{8,10},{9,11},{10,... | collective-permute-start | bytes 331784 | tf_op jit(solution)/shard_map/ppermute | solution.py:562
  341.5 29.4 %collective-permute-start.24 = (bf16[48,1152]{1,0:T(8,128)(2,1)S(1)}, bf16[48,1152]{1,0:T(8,128)(2,1)S(1)}, u32[]{:S(2)}, u32[]{:S(2)}) collective-permute-start(bf16[48,1152]{1,0:T(8,128)(2,1)S(1)} %fusion.12), channel_id=1, source_target_pairs={{0,1},{1,0},{2,3},{3,2},{4,5},{5,4},{6,7},{7,6},{8,9},{9,8},{10,11... | collective-permute-start | bytes 331784 | tf_op jit(solution)/shard_map/ppermute | solution.py:562
  341.5 29.4 %collective-permute-start.25 = (bf16[48,1152]{1,0:T(8,128)(2,1)S(1)}, bf16[48,1152]{1,0:T(8,128)(2,1)S(1)}, u32[]{:S(2)}, u32[]{:S(2)}) collective-permute-start(bf16[48,1152]{1,0:T(8,128)(2,1)S(1)} %fusion.12), channel_id=1, source_target_pairs={{0,3},{1,2},{2,1},{3,0},{4,7},{5,6},{6,5},{7,4},{8,11},{9,10},{10,... | collective-permute-start | bytes 331784 | tf_op jit(solution)/shard_map/ppermute | solution.py:562
  368.8 12.7 %collective-permute-start.33 = (bf16[4,48,1920]{2,1,0:T(8,128)(2,1)S(1)}, bf16[4,48,1920]{2,1,0:T(8,128)(2,1)S(1)}, u32[]{:S(2)}, u32[]{:S(2)}) collective-permute-start(bf16[4,48,1920]{2,1,0:T(8,128)(2,1)S(1)} %get-tuple-element.70), channel_id=1, source_target_pairs={{0,4},{4,0},{8,12},{12,8},{16,20},{20,16},{24,28},{28,24},{1,5},{5... | collective-permute-start | bytes 2211848 | tf_op jit(solution)/shard_map/ppermute | solution.py:562
  370.5 9.3 %collective-permute-start.42 = (bf16[2,96,768]{2,1,0:T(8,128)(2,1)S(1)}, bf16[2,96,768]{2,1,0:T(8,128)(2,1)S(1)}, u32[]{:S(2)}, u32[]{:S(2)}) collective-permute-start(bf16[2,96,768]{2,1,0:T(8,128)(2,1)S(1)} %get-tuple-element.78), channel_id=1, source_target_pairs={{0,8},{4,12},{8,0},{12,4},{16,24},{20,28},{24,16},{28,20},{1,9},{5... | collective-permute-start | bytes 884744 | tf_op jit(solution)/shard_map/ppermute | solution.py:562
  380.6 7.6 %collective-permute-start.43 = (bf16[1,96,768]{2,1,0:T(8,128)(2,1)}, bf16[1,96,768]{2,1,0:T(8,128)(2,1)}, u32[]{:S(2)}, u32[]{:S(2)}) collective-permute-start(bf16[1,96,768]{2,1,0:T(8,128)(2,1)} %add_convert_fusion.16), channel_id=1, source_target_pairs={{0,16},{4,20},{8,24},{12,28},{16,0},{20,4},{24,8},{28,12},{1,17},{... | collective-permute-start | bytes 442376 | tf_op jit(solution)/shard_map/ppermute | solution.py:562
  381.6 9.7 %collective-permute-start.34 = (bf16[2,48,1920]{2,1,0:T(8,128)(2,1)S(1)}, bf16[2,48,1920]{2,1,0:T(8,128)(2,1)S(1)}, u32[]{:S(2)}, u32[]{:S(2)}) collective-permute-start(bf16[2,48,1920]{2,1,0:T(8,128)(2,1)S(1)} %get-tuple-element.76), channel_id=1, source_target_pairs={{0,8},{4,12},{8,0},{12,4},{16,24},{20,28},{24,16},{28,20},{1,9},{5... | collective-permute-start | bytes 1105928 | tf_op jit(solution)/shard_map/ppermute | solution.py:562
  389.1 5.9 %collective-permute-start.44 = (bf16[96,768]{1,0:T(8,128)(2,1)S(1)}, bf16[96,768]{1,0:T(8,128)(2,1)S(1)}, u32[]{:S(2)}, u32[]{:S(2)}) collective-permute-start(bf16[96,768]{1,0:T(8,128)(2,1)S(1)} %fusion.11), channel_id=1, source_target_pairs={{0,2},{1,3},{2,0},{3,1},{4,6},{5,7},{6,4},{7,5},{8,10},{9,11},{10,... | collective-permute-start | bytes 442376 | tf_op jit(solution)/shard_map/ppermute | solution.py:562
  390.7 4.4 %collective-permute-start.45 = (bf16[96,768]{1,0:T(8,128)(2,1)S(1)}, bf16[96,768]{1,0:T(8,128)(2,1)S(1)}, u32[]{:S(2)}, u32[]{:S(2)}) collective-permute-start(bf16[96,768]{1,0:T(8,128)(2,1)S(1)} %fusion.11), channel_id=1, source_target_pairs={{0,1},{1,0},{2,3},{3,2},{4,5},{5,4},{6,7},{7,6},{8,9},{9,8},{10,11... | collective-permute-start | bytes 442376 | tf_op jit(solution)/shard_map/ppermute | solution.py:562
  390.7 6.1 %collective-permute-start.46 = (bf16[96,768]{1,0:T(8,128)(2,1)S(1)}, bf16[96,768]{1,0:T(8,128)(2,1)S(1)}, u32[]{:S(2)}, u32[]{:S(2)}) collective-permute-start(bf16[96,768]{1,0:T(8,128)(2,1)S(1)} %fusion.11), channel_id=1, source_target_pairs={{0,3},{1,2},{2,1},{3,0},{4,7},{5,6},{6,5},{7,4},{8,11},{9,10},{10,... | collective-permute-start | bytes 442376 | tf_op jit(solution)/shard_map/ppermute | solution.py:562
  391.4 9.9 %collective-permute-start.35 = (bf16[1,48,1920]{2,1,0:T(8,128)(2,1)S(1)}, bf16[1,48,1920]{2,1,0:T(8,128)(2,1)S(1)}, u32[]{:S(2)}, u32[]{:S(2)}) collective-permute-start(bf16[1,48,1920]{2,1,0:T(8,128)(2,1)S(1)} %add_convert_fusion.13), channel_id=1, source_target_pairs={{0,16},{4,20},{8,24},{12,28},{16,0},{20,4},{24,8},{28,12},{1,17},{... | collective-permute-start | bytes 552968 | tf_op jit(solution)/shard_map/ppermute | solution.py:562
  401.3 7.6 %collective-permute-start.36 = (bf16[48,1920]{1,0:T(8,128)(2,1)S(1)}, bf16[48,1920]{1,0:T(8,128)(2,1)S(1)}, u32[]{:S(2)}, u32[]{:S(2)}) collective-permute-start(bf16[48,1920]{1,0:T(8,128)(2,1)S(1)} %fusion.10), channel_id=1, source_target_pairs={{0,2},{1,3},{2,0},{3,1},{4,6},{5,7},{6,4},{7,5},{8,10},{9,11},{10,... | collective-permute-start | bytes 552968 | tf_op jit(solution)/shard_map/ppermute | solution.py:562
  402.9 6.0 %collective-permute-start.37 = (bf16[48,1920]{1,0:T(8,128)(2,1)S(1)}, bf16[48,1920]{1,0:T(8,128)(2,1)S(1)}, u32[]{:S(2)}, u32[]{:S(2)}) collective-permute-start(bf16[48,1920]{1,0:T(8,128)(2,1)S(1)} %fusion.10), channel_id=1, source_target_pairs={{0,1},{1,0},{2,3},{3,2},{4,5},{5,4},{6,7},{7,6},{8,9},{9,8},{10,11... | collective-permute-start | bytes 552968 | tf_op jit(solution)/shard_map/ppermute | solution.py:562
  402.9 8.1 %collective-permute-start.38 = (bf16[48,1920]{1,0:T(8,128)(2,1)S(1)}, bf16[48,1920]{1,0:T(8,128)(2,1)S(1)}, u32[]{:S(2)}, u32[]{:S(2)}) collective-permute-start(bf16[48,1920]{1,0:T(8,128)(2,1)S(1)} %fusion.10), channel_id=1, source_target_pairs={{0,3},{1,2},{2,1},{3,0},{4,7},{5,6},{6,5},{7,4},{8,11},{9,10},{10,... | collective-permute-start | bytes 552968 | tf_op jit(solution)/shard_map/ppermute | solution.py:562
  (8 other events, 33.6 us)
